TPU v7x, 256 devices: a whole 4x4x8 slice. The times are simulated.
256 devices in a mesh: lat: 4 (over z_hi), lon: 64 (over x, z_lo, y, core).
Axes of the slice: x: 4, y: 4, z: 8 (z_hi: 4, z_lo: 2; z = z_hi * 2 + z_lo), core: 2. Of those that a mesh axis runs over, the one named last changes fastest.
Arguments:
- ensemble: float32 [2, 32, 128, 16384], P(None, None, 'lat', 'lon'), may hold values from -6 to 6
- courant_x: float32 [128, 16384], P('lat', 'lon'), may hold values from -0.2 to 0.2
- courant_y: float32 [128, 16384], P('lat', 'lon'), may hold values from -0.2 to 0.2
- diffusion: float32 [2], replicated, may hold values from 0.03 to 0.12
- obs_cell: int32 [2, 1024], replicated, may hold values from 0 to 2097151, as said below
- obs_value: float32 [2, 1024], replicated, may hold values from -6 to 6
- obs_noise: float32 [2, 1024, 32], replicated, may hold values from -4 to 4
- obs_var: float32 [2, 1024], replicated, may hold values from 0.3 to 1.5
- loc_mask: int32 [4, 64, 2, 1024], P('lat', 'lon'), may hold values from 0 to 1, as said below
Outputs:
- analysis: float32 [2, 32, 128, 16384], P(None, None, 'lat', 'lon')
Inputs may be any that keep to these rules, and one draw needn't show every extreme that they name: `obs_cell`: no tile of 32 x 256 cells holds more than 16 of one batch's observations; some tile holds exactly 16 in every batch. `loc_mask`: 1 exactly where the tile is at most one tile row and at most 2 tile columns (periodically) from the tile of the observation's cell, else 0.
All inputs are finite; a program needn't handle non-finite values.
Results may differ from a plain program's by a relative error of at most 0.0003.
Values sent between devices are 32-bit elements; how exact they have to be, the bound alone decides.
A program may use at most 64 MiB of HBM per device.

v0:
```python
import jax
import jax.numpy as jnp
from jax import lax
from jax.sharding import PartitionSpec as P

LOCR = 2
SLOTS = 16


def extended(block, sides, width, periodic):
    for axis, dim in sides:
        count = lax.axis_size(axis)
        forward = [(i, i + 1) for i in range(count - 1)]
        if periodic:
            forward.append((count - 1, 0))
        backward = [(target, source) for source, target in forward]
        low = lax.ppermute(
            lax.slice_in_dim(block, block.shape[dim] - width, None, axis=dim), axis, forward
        )
        high = lax.ppermute(lax.slice_in_dim(block, 0, width, axis=dim), axis, backward)
        block = jnp.concatenate([low, block, high], axis=dim)
    return block


def from_behind(x, axis, by):
    length = lax.axis_size(axis)
    return lax.ppermute(x, axis, [(i, (i + by) % length) for i in range(length)])


def combine_terms(
    center, west_side, east_side, south_side, north_side, courant_x, courant_y, diff_rate
):
    out = (
        center
        - jnp.maximum(courant_x, 0.0) * (center - west_side)
        - jnp.minimum(courant_x, 0.0) * (east_side - center)
    )
    out = (
        out
        - jnp.maximum(courant_y, 0.0) * (center - south_side)
        - jnp.minimum(courant_y, 0.0) * (north_side - center)
    )
    return out + diff_rate * (west_side + east_side + south_side + north_side - 4.0 * center)


def advance(ensemble, courant_x, courant_y, diffusion):
    row_ext = extended(ensemble, (("lat", 2),), 1, False)
    col_ext = extended(ensemble, (("lon", 3),), 1, True)
    return combine_terms(
        ensemble,
        col_ext[:, :, :, :-2],
        col_ext[:, :, :, 2:],
        row_ext[:, :, :-2, :],
        row_ext[:, :, 2:, :],
        courant_x,
        courant_y,
        diffusion[:, None, None, None],
    )


def transform_of(spread, innovation, weight):
    members = spread.shape[1]
    weighted = spread * weight[:, None]
    system = (members - 1.0) * jnp.eye(members, dtype=jnp.float32) + jnp.dot(
        spread.T, weighted, precision=lax.Precision.HIGHEST
    )
    right_side = jnp.dot(weighted.T, innovation, precision=lax.Precision.HIGHEST)
    factor = jnp.linalg.cholesky(system)
    return jax.scipy.linalg.cho_solve((factor, True), right_side)


def slot_table(cells, row_count, col_count, lat_count, lon_count, slot_count):
    grid_width = col_count * lon_count
    tile_of = cells // grid_width // row_count * lon_count + cells % grid_width // col_count
    order = jnp.arange(cells.shape[0], dtype=jnp.int32)
    earlier = (tile_of[None, :] == tile_of[:, None]) & (order[None, :] < order[:, None])
    rank = jnp.sum(earlier.astype(jnp.int32), axis=1)
    table = jnp.full((lat_count * lon_count * slot_count,), -1, jnp.int32)
    table = table.at[tile_of * slot_count + rank].set(order, mode="drop")
    return table.reshape(lat_count, lon_count, slot_count)


def local(
    ensemble, courant_x, courant_y, diffusion, obs_cell, obs_value, obs_noise, obs_var, loc_mask
):
    for substep in range(2):
        ensemble = advance(ensemble, courant_x, courant_y, diffusion)
    lat_index = lax.axis_index("lat")
    lon_index = lax.axis_index("lon")
    lat_count = lax.axis_size("lat")
    lon_count = lax.axis_size("lon")
    row_count = ensemble.shape[2]
    col_count = ensemble.shape[3]
    members = ensemble.shape[1]
    grid_width = col_count * lon_count
    slot_count = SLOTS
    for batch_index in range(obs_cell.shape[0]):
        observed_field = batch_index % ensemble.shape[0]
        id_table = slot_table(
            obs_cell[batch_index], row_count, col_count, lat_count, lon_count, slot_count
        )
        own_ids = lax.dynamic_slice(
            id_table, (lat_index, lon_index, jnp.int32(0)), (1, 1, slot_count)
        )[0, 0]
        own_valid = own_ids >= 0
        flat_cell = obs_cell[batch_index][jnp.where(own_valid, own_ids, 0)]
        local_row = jnp.where(own_valid, flat_cell // grid_width - lat_index * row_count, 0)
        local_col = jnp.where(own_valid, flat_cell % grid_width - lon_index * col_count, 0)
        priors = ensemble[observed_field][:, local_row, local_col].T
        priors = jnp.where(own_valid[:, None], priors, 0.0)
        pieces = []
        for offset in range(-LOCR, LOCR + 1):
            if offset == 0:
                pieces.append(priors)
            else:
                pieces.append(from_behind(priors, "lon", -offset))
        nearby = jnp.stack(pieces, axis=0)[None]
        nearby = extended(nearby, (("lat", 0),), 1, False)
        lat_rows = lat_index + jnp.arange(-1, 2, dtype=jnp.int32)
        lon_cols = (lon_index + jnp.arange(-LOCR, LOCR + 1, dtype=jnp.int32)) % lon_count
        inside = (lat_rows >= 0) & (lat_rows < lat_count)
        picked = id_table[jnp.clip(lat_rows, 0, lat_count - 1)][:, lon_cols]
        slot_ids = jnp.where(inside[:, None, None], picked, -1).reshape(-1)
        received = nearby.reshape(-1, members)
        present = slot_ids >= 0
        safe_ids = jnp.where(present, slot_ids, 0)
        mask_row = loc_mask[0, 0, batch_index][safe_ids].astype(jnp.float32)
        weight = jnp.where(present, mask_row / obs_var[batch_index][safe_ids], 0.0)
        spread = received - jnp.mean(received, axis=1, keepdims=True)
        innovation = (
            obs_value[batch_index][safe_ids][:, None] + obs_noise[batch_index][safe_ids] - received
        )
        transform = transform_of(spread, innovation, weight)
        anomaly = ensemble - jnp.mean(ensemble, axis=1, keepdims=True)
        ensemble = ensemble + jnp.einsum(
            "fmyx,mk->fkyx", anomaly, transform, precision=lax.Precision.HIGHEST
        )
    return ensemble


def solution(mesh):
    in_specs = (
        P(None, None, "lat", "lon"),
        P("lat", "lon"),
        P("lat", "lon"),
        P(),
        P(),
        P(),
        P(),
        P(),
        P("lat", "lon", None, None),
    )
    out_specs = P(None, None, "lat", "lon")
    return jax.shard_map(local, mesh=mesh, in_specs=in_specs, out_specs=out_specs, check_vma=False)
```

profile of v0, /device:TPU:1, one launch (start us, length us, event | category | flops | bytes accessed | tf_op | source)
XLA Modules:
  0.0 164.7 jit_solution(12901595484328190011)
XLA Ops:
  0.0 3.0 %copy.142 = f32[2,32,32,256]{3,1,2,0:T(8,128)S(1)} copy(f32[2,32,32,256]{3,2,1,0:T(8,128)} %param.12) | data formatting | bytes 4194304 | tf_op args[0]
  3.0 0.7 fusion.122
  3.7 6.3 %collective-permute-start.2 = (f32[2,32,1,256]{3,1,2,0:T(8,128)}, f32[2,32,1,256]{3,1,2,0:T(8,128)}, u32[]{:S(2)}, u32[]{:S(2)}) collective-permute-start(f32[2,32,1,256]{3,1,2,0:T(8,128)} %get-tuple-element.19), channel_id=1, source_target_pairs={{0,64},{64,128},{128,192},{1,65},{65,129},{129,193},{2,66},{66,130... | collective-permute-start | bytes 196616 | tf_op jit(solution)/shard_map/ppermute | solution.py:17
  10.0 1.3 collective-permute-start.3
  12.1 2.2 %collective-permute-start = (f32[2,32,32,1]{2,1,3,0:T(8,128)S(1)}, f32[2,32,32,1]{2,1,3,0:T(8,128)S(1)}, u32[]{:S(2)}, u32[]{:S(2)}) collective-permute-start(f32[2,32,32,1]{2,1,3,0:T(8,128)S(1)} %copy.189), channel_id=1, source_target_pairs={{0,1},{1,2},{2,3},{3,4},{4,5},{5,6},{6,7},{7,8},{8,9},{9,10},{10,1... | collective-permute-start | bytes 24584 | tf_op jit(solution)/shard_map/ppermute | solution.py:17
  16.3 4.3 %scatter_custom_fusion = s32[4096]{0:T(1024)S(1)} fusion(s32[1024]{0:T(1024)S(1)} %bitcast.221, s32[1024]{0:T(1024)S(1)} %iota.77, s32[]{:T(128)} %constant.190.clone.1), kind=kCustom, calls=%fused_computation.206 | custom fusion | bytes 16388 | tf_op jit(solution)/shard_map/scatter | solution.py:79
  20.8 4.5 %scatter_custom_fusion.1 = s32[4096]{0:T(1024)S(1)} fusion(s32[1024]{0:T(1024)S(1)} %bitcast.216, s32[1024]{0:T(1024)S(1)} %iota.81, s32[]{:T(128)} %constant.190.clone.1), kind=kCustom, calls=%fused_computation.204 | custom fusion | bytes 16388 | tf_op jit(solution)/shard_map/scatter | solution.py:79
  25.6 0.6 compare_bitcast_fusion
  26.2 0.6 gather_fusion
  30.1 1.4 gather_fusion.4
  31.5 1.4 gather_fusion.5
  33.0 0.6 copy_select_fusion.1
  33.6 1.4 gather_fusion.12
  35.0 1.4 gather_fusion.13
  37.6 0.9 copy.139
  38.6 1.8 %copy.145 = f32[2,32,32,1]{3,1,2,0:T(8,128)} copy(f32[2,32,32,1]{2,1,3,0:T(8,128)S(1)} %collective-permute-done.1) | data formatting | bytes 16384 | tf_op jit(solution)/shard_map/ppermute | solution.py:20
  40.4 6.4 %fusion.24 = f32[2,32,32,256]{3,1,2,0:T(8,128)S(1)} fusion(f32[2,32,1,256]{3,1,2,0:T(8,128)} %collective-permute-done.3, f32[2,32,32,256]{3,1,2,0:T(8,128)} %copy-done.4, f32[2,32,1,256]{3,1,2,0:T(8,128)} %collective-permute-done.2, f32[2,32,32,1]{3,1,2,0:T(8,128)} %copy.145, f32[2,32,32,1]{3,1,2,0:T(8,128)S(1)} %copy.139, f32[2]{0:T(128)} %param.15, ...), kind=kLoop, calls=%fused_computation.50 | loop fusion | flops 12058624 | bytes 4472840 | tf_op jit(solution)/shard_map/add | solution.py:43
  46.8 1.4 fusion.119
  48.2 0.7 fusion.120
  48.9 2.4 %copy.154 = f32[2,32,32,1]{2,1,3,0:T(8,128)} copy(f32[2,32,32,1]{3,1,2,0:T(8,128)} %get-tuple-element.13) | data formatting | bytes 16384 | tf_op jit(solution)/shard_map/slice | solution.py:18
  51.2 1.7 %collective-permute-start.4 = (f32[2,32,32,1]{2,1,3,0:T(8,128)}, f32[2,32,32,1]{2,1,3,0:T(8,128)}, u32[]{:S(2)}, u32[]{:S(2)}) collective-permute-start(f32[2,32,32,1]{2,1,3,0:T(8,128)} %copy.154), channel_id=1, source_target_pairs={{0,1},{1,2},{2,3},{3,4},{4,5},{5,6},{6,7},{7,8},{8,9},{9,10},{10,1... | collective-permute-start | bytes 24584 | tf_op jit(solution)/shard_map/ppermute | solution.py:17
  52.9 1.3 copy.156
  54.2 3.0 %collective-permute-start.5 = (f32[2,32,32,1]{2,1,3,0:T(8,128)}, f32[2,32,32,1]{2,1,3,0:T(8,128)}, u32[]{:S(2)}, u32[]{:S(2)}) collective-permute-start(f32[2,32,32,1]{2,1,3,0:T(8,128)} %copy.156), channel_id=1, source_target_pairs={{1,0},{2,1},{3,2},{4,3},{5,4},{6,5},{7,6},{8,7},{9,8},{10,9},{11,1... | collective-permute-start | bytes 24584 | tf_op jit(solution)/shard_map/ppermute | solution.py:20
  57.3 6.8 %collective-permute-start.6 = (f32[2,32,1,256]{3,1,2,0:T(8,128)}, f32[2,32,1,256]{3,1,2,0:T(8,128)}, u32[]{:S(2)}, u32[]{:S(2)}) collective-permute-start(f32[2,32,1,256]{3,1,2,0:T(8,128)} %get-tuple-element.15), channel_id=1, source_target_pairs={{0,64},{64,128},{128,192},{1,65},{65,129},{129,193},{2,66},{66,130... | collective-permute-start | bytes 196616 | tf_op jit(solution)/shard_map/ppermute | solution.py:17
  64.0 1.3 collective-permute-start.7
  65.3 0.7 pad_clamp_fusion.1
  66.0 1.1 gather_fusion.8
  67.1 1.7 %copy.155 = f32[2,32,32,1]{3,1,2,0:T(8,128)S(1)} copy(f32[2,32,32,1]{2,1,3,0:T(8,128)} %collective-permute-done.4) | data formatting | bytes 16384 | tf_op jit(solution)/shard_map/ppermute | solution.py:17
  68.8 2.6 %copy.157 = f32[2,32,32,1]{3,1,2,0:T(8,128)} copy(f32[2,32,32,1]{2,1,3,0:T(8,128)} %collective-permute-done.5) | data formatting | bytes 16384 | tf_op jit(solution)/shard_map/ppermute | solution.py:20
  71.4 4.6 %fusion.117 = (f32[2,32,256]{2,1,0:T(8,128)}, f32[2,32,32,256]{3,1,2,0:T(8,128)S(1)}) fusion(f32[2,32,32,256]{3,1,2,0:T(8,128)S(1)} %fusion.24, f32[2]{0:T(128)} %param.15, f32[2,32,1,256]{3,1,2,0:T(8,128)} %collective-permute-done.7, f32[32,256]{1,0:T(8,128)S(1)} %get-tuple-element.26, f32[2,32,1,256]{3,1,2,0:T(8,128)} %collective-permute-done.6, ...), kind=kLoop, calls=%fused_computation.325 | loop fusion | flops 12566528 | bytes 4538376 | tf_op jit(solution)/shard_map/reduce_sum | solution.py:134
  76.0 1.3 copy-done
  77.5 2.7 %copy.158 = f32[32,32,256]{0,2,1:T(8,128)} copy(f32[32,32,256]{2,0,1:T(8,128)S(1)} %slice_bitcast_fusion.1) | data formatting | bytes 2097152 | tf_op jit(solution)/shard_map/squeeze | solution.py:109
  80.1 1.7 %gather_fusion.1 = f32[16,32]{1,0:T(8,128)S(1)} fusion(f32[32,32,256]{0,2,1:T(8,128)} %copy.158, s32[16]{0:T(128)S(1)} %or_bitcast_fusion.1), kind=kCustom, calls=%fused_computation.1 | custom fusion | bytes 4224 | tf_op jit(solution)/shard_map/gather | solution.py:109
  82.2 0.7 gather_fusion.7
  83.0 1.4 gather_fusion.6
  84.5 2.2 %collective-permute-start.9 = (f32[16,32]{1,0:T(8,128)S(1)}, f32[16,32]{1,0:T(8,128)S(1)}, u32[]{:S(2)}, u32[]{:S(2)}) collective-permute-start(f32[16,32]{1,0:T(8,128)S(1)} %broadcast_select_fusion.1), channel_id=1, source_target_pairs={{0,1},{1,2},{2,3},{3,4},{4,5},{5,6},{6,7},{7,8},{8,9},{9,10},{10,1... | collective-permute-start | bytes 6152 | tf_op jit(solution)/shard_map/ppermute | solution.py:27
  86.6 5.0 %collective-permute-start.10 = (f32[16,32]{1,0:T(8,128)S(1)}, f32[16,32]{1,0:T(8,128)S(1)}, u32[]{:S(2)}, u32[]{:S(2)}) collective-permute-start(f32[16,32]{1,0:T(8,128)S(1)} %broadcast_select_fusion.1), channel_id=1, source_target_pairs={{0,63},{1,0},{2,1},{3,2},{4,3},{5,4},{6,5},{7,6},{8,7},{9,8},{10,9... | collective-permute-start | bytes 6152 | tf_op jit(solution)/shard_map/ppermute | solution.py:27
  91.7 5.9 %collective-permute-start.11 = (f32[16,32]{1,0:T(8,128)S(1)}, f32[16,32]{1,0:T(8,128)S(1)}, u32[]{:S(2)}, u32[]{:S(2)}) collective-permute-start(f32[16,32]{1,0:T(8,128)S(1)} %broadcast_select_fusion.1), channel_id=1, source_target_pairs={{0,62},{1,63},{2,0},{3,1},{4,2},{5,3},{6,4},{7,5},{8,6},{9,7},{10,... | collective-permute-start | bytes 6152 | tf_op jit(solution)/shard_map/ppermute | solution.py:27
  97.7 0.7 collective-permute-done.11
  98.4 5.7 %collective-permute-start.12 = (f32[1,5,16,32]{3,2,1,0:T(8,128)S(1)}, f32[1,5,16,32]{3,2,1,0:T(8,128)S(1)}, u32[]{:S(2)}, u32[]{:S(2)}) collective-permute-start(f32[1,5,16,32]{3,2,1,0:T(8,128)S(1)} %bitcast.204), channel_id=1, source_target_pairs={{0,64},{64,128},{128,192},{1,65},{65,129},{129,193},{2,66},{66,130... | collective-permute-start | bytes 30728 | tf_op jit(solution)/shard_map/ppermute | solution.py:17
  104.1 1.3 collective-permute-start.13
  105.5 5.2 %collective-permute-done.13 = f32[1,5,16,32]{3,2,1,0:T(8,128)S(1)} collective-permute-done((f32[1,5,16,32]{3,2,1,0:T(8,128)S(1)}, f32[1,5,16,32]{3,2,1,0:T(8,128)S(1)}, u32[]{:S(2)}, u32[]{:S(2)}) %collective-permute-start.13) | collective-permute-done | bytes 10272 | tf_op jit(solution)/shard_map/ppermute | solution.py:20
  111.4 2.9 %cholesky.44 = f32[32,32]{1,0:T(8,128)S(1)} custom-call(f32[32,32]{1,0:T(8,128)S(1)} %fusion.83), custom_call_target="Cholesky" | custom-call | tf_op jit(solution)/shard_map/jit(cholesky)/cholesky | solution.py:68
  114.3 0.6 compare_reduce_fusion.1
  115.6 2.4 %custom-call.12 = f32[1,32,32]{1,2,0:T(8,128)S(1)} custom-call(f32[1,32,32]{2,1,0:T(8,128)S(1)} %fusion.74), custom_call_target="InvertDiagBlocksLowerTriangular" | custom-call | tf_op jit(solution)/shard_map/jit(_cho_solve)/triangular_solve | solution.py:69
  119.0 2.1 %fusion.128 = (f32[2,32,256]{2,1,0:T(8,128)S(1)}, f32[2,32,32,256]{3,1,2,0:T(8,128)S(1)}) fusion(f32[2,32,32,256]{3,1,2,0:T(8,128)S(1)} %copy-done.1, f32[32,32,1,1]{0,1,3,2:T(8,128)S(1)} %convolution_bitcast_fusion.3, f32[2,32,256]{2,1,0:T(8,128)S(1)} %broadcast_multiply_fusion.1), kind=kOutput, calls=%fused_computation.335 | convolution fusion | flops 202883072 | bytes 4329472 | tf_op jit(solution)/shard_map/fmyx,mk->fkyx/dot_general | solution.py:135
  121.0 1.3 copy-done.2
  122.4 2.7 %copy.168 = f32[32,32,256]{0,2,1:T(8,128)} copy(f32[32,32,256]{2,0,1:T(8,128)S(1)} %slice_bitcast_fusion) | data formatting | bytes 2097152 | tf_op jit(solution)/shard_map/squeeze | solution.py:109
  125.1 1.7 %gather_fusion.9 = f32[16,32]{1,0:T(8,128)S(1)} fusion(f32[32,32,256]{0,2,1:T(8,128)} %copy.168, s32[16]{0:T(128)S(1)} %or_bitcast_fusion), kind=kCustom, calls=%fused_computation.9 | custom fusion | bytes 4224 | tf_op jit(solution)/shard_map/gather | solution.py:109
  127.2 0.7 gather_fusion.15
  127.9 1.4 gather_fusion.14
  129.3 2.9 %collective-permute-start.15 = (f32[16,32]{1,0:T(8,128)S(1)}, f32[16,32]{1,0:T(8,128)S(1)}, u32[]{:S(2)}, u32[]{:S(2)}) collective-permute-start(f32[16,32]{1,0:T(8,128)S(1)} %broadcast_select_fusion), channel_id=1, source_target_pairs={{0,1},{1,2},{2,3},{3,4},{4,5},{5,6},{6,7},{7,8},{8,9},{9,10},{10,1... | collective-permute-start | bytes 6152 | tf_op jit(solution)/shard_map/ppermute | solution.py:27
  132.2 1.1 collective-permute-start.16
  133.4 6.3 %collective-permute-start.17 = (f32[16,32]{1,0:T(8,128)S(1)}, f32[16,32]{1,0:T(8,128)S(1)}, u32[]{:S(2)}, u32[]{:S(2)}) collective-permute-start(f32[16,32]{1,0:T(8,128)S(1)} %broadcast_select_fusion), channel_id=1, source_target_pairs={{0,62},{1,63},{2,0},{3,1},{4,2},{5,3},{6,4},{7,5},{8,6},{9,7},{10,... | collective-permute-start | bytes 6152 | tf_op jit(solution)/shard_map/ppermute | solution.py:27
  139.8 0.7 collective-permute-done.17
  140.5 5.8 %collective-permute-start.18 = (f32[1,5,16,32]{3,2,1,0:T(8,128)S(1)}, f32[1,5,16,32]{3,2,1,0:T(8,128)S(1)}, u32[]{:S(2)}, u32[]{:S(2)}) collective-permute-start(f32[1,5,16,32]{3,2,1,0:T(8,128)S(1)} %bitcast.209), channel_id=1, source_target_pairs={{0,64},{64,128},{128,192},{1,65},{65,129},{129,193},{2,66},{66,130... | collective-permute-start | bytes 30728 | tf_op jit(solution)/shard_map/ppermute | solution.py:17
  146.3 1.6 collective-permute-start.19
  147.9 4.1 %collective-permute-done.19 = f32[1,5,16,32]{3,2,1,0:T(8,128)S(1)} collective-permute-done((f32[1,5,16,32]{3,2,1,0:T(8,128)S(1)}, f32[1,5,16,32]{3,2,1,0:T(8,128)S(1)}, u32[]{:S(2)}, u32[]{:S(2)}) %collective-permute-start.19) | collective-permute-done | bytes 10272 | tf_op jit(solution)/shard_map/ppermute | solution.py:20
  152.6 2.9 %cholesky.55 = f32[32,32]{1,0:T(8,128)S(1)} custom-call(f32[32,32]{1,0:T(8,128)S(1)} %fusion.79), custom_call_target="Cholesky" | custom-call | tf_op jit(solution)/shard_map/jit(cholesky)/cholesky | solution.py:68
  155.6 0.7 compare_reduce_fusion
  156.2 0.6 fusion.75
  156.9 2.4 %custom-call.13 = f32[1,32,32]{1,2,0:T(8,128)S(1)} custom-call(f32[1,32,32]{2,1,0:T(8,128)S(1)} %fusion.75), custom_call_target="InvertDiagBlocksLowerTriangular" | custom-call | tf_op jit(solution)/shard_map/jit(_cho_solve)/triangular_solve | solution.py:69
  160.3 1.9 %bitcast_add_fusion = f32[2,32,32,256]{3,1,2,0:T(8,128)S(1)} fusion(f32[2,32,32,256]{3,1,2,0:T(8,128)S(1)} %copy-done.3, f32[32,32,1,1]{0,1,3,2:T(8,128)S(1)} %convolution_bitcast_fusion, f32[2,32,256]{2,1,0:T(8,128)S(1)} %broadcast_multiply_fusion), kind=kOutput, calls=%fused_computation.67 | convolution fusion | flops 202375168 | bytes 4263936 | tf_op jit(solution)/shard_map/fmyx,mk->fkyx/dot_general | solution.py:135
  162.2 2.5 %copy.178 = f32[2,32,32,256]{3,2,1,0:T(8,128)} copy(f32[2,32,32,256]{3,1,2,0:T(8,128)S(1)} %bitcast_add_fusion) | data formatting | bytes 4194304 | tf_op jit(solution)/shard_map/add | solution.py:135
  (161 shorter events, 12.7 us)
Async XLA Ops:
  0.0 11.3 %copy-start.5 = (f32[2,32,32,256]{3,2,1,0:T(8,128)S(1)}, f32[2,32,32,256]{3,2,1,0:T(8,128)}, u32[]{:S(2)}) copy-start(f32[2,32,32,256]{3,2,1,0:T(8,128)} %param.12) | copy-start | bytes 6291460
  3.0 8.7 %copy-start.4 = (f32[2,32,32,256]{3,1,2,0:T(8,128)}, f32[2,32,32,256]{3,1,2,0:T(8,128)S(1)}, u32[]{:S(2)}) copy-start(f32[2,32,32,256]{3,1,2,0:T(8,128)S(1)} %copy.142) | copy-start | bytes 6291460
  3.7 36.7 %collective-permute-start.2 = (f32[2,32,1,256]{3,1,2,0:T(8,128)}, f32[2,32,1,256]{3,1,2,0:T(8,128)}, u32[]{:S(2)}, u32[]{:S(2)}) collective-permute-start(f32[2,32,1,256]{3,1,2,0:T(8,128)} %get-tuple-element.19), channel_id=1, source_target_pairs={{0,64},{64,128},{128,192},{1,65},{65,129},{129,193},{2,66},{66,130... | collective-permute-start | bytes 196616 | tf_op jit(solution)/shard_map/ppermute | solution.py:17
  10.0 30.4 %collective-permute-start.3 = (f32[2,32,1,256]{3,1,2,0:T(8,128)}, f32[2,32,1,256]{3,1,2,0:T(8,128)}, u32[]{:S(2)}, u32[]{:S(2)}) collective-permute-start(f32[2,32,1,256]{3,1,2,0:T(8,128)} %get-tuple-element.20), channel_id=1, source_target_pairs={{64,0},{128,64},{192,128},{65,1},{129,65},{193,129},{66,2},{130,66... | collective-permute-start | bytes 196616 | tf_op jit(solution)/shard_map/ppermute | solution.py:20
  11.7 3.2 %copy-start.11 = (s32[2,1024]{1,0:T(2,128)S(1)}, s32[2,1024]{1,0:T(2,128)}, u32[]{:S(2)}) copy-start(s32[2,1024]{1,0:T(2,128)} %param.16) | copy-start | bytes 24580
  11.7 18.3 %copy-start.18 = (s32[1,1,2,1024]{3,2,1,0:T(2,128)S(1)}, s32[1,1,2,1024]{3,2,1,0:T(2,128)}, u32[]{:S(2)}) copy-start(s32[1,1,2,1024]{3,2,1,0:T(2,128)} %param.20) | copy-start | bytes 24580
  11.7 18.3 %copy-start.19 = (f32[2,1024]{1,0:T(2,128)S(1)}, f32[2,1024]{1,0:T(2,128)}, u32[]{:S(2)}) copy-start(f32[2,1024]{1,0:T(2,128)} %param.19) | copy-start | bytes 24580
  12.1 25.5 %collective-permute-start = (f32[2,32,32,1]{2,1,3,0:T(8,128)S(1)}, f32[2,32,32,1]{2,1,3,0:T(8,128)S(1)}, u32[]{:S(2)}, u32[]{:S(2)}) collective-permute-start(f32[2,32,32,1]{2,1,3,0:T(8,128)S(1)} %copy.189), channel_id=1, source_target_pairs={{0,1},{1,2},{2,3},{3,4},{4,5},{5,6},{6,7},{7,8},{8,9},{9,10},{10,1... | collective-permute-start | bytes 24584 | tf_op jit(solution)/shard_map/ppermute | solution.py:17
  14.8 23.8 %collective-permute-start.1 = (f32[2,32,32,1]{2,1,3,0:T(8,128)S(1)}, f32[2,32,32,1]{2,1,3,0:T(8,128)S(1)}, u32[]{:S(2)}, u32[]{:S(2)}) collective-permute-start(f32[2,32,32,1]{2,1,3,0:T(8,128)S(1)} %copy.190), channel_id=1, source_target_pairs={{1,0},{2,1},{3,2},{4,3},{5,4},{6,5},{7,6},{8,7},{9,8},{10,9},{11,1... | collective-permute-start | bytes 24584 | tf_op jit(solution)/shard_map/ppermute | solution.py:20
  20.8 12.8 %copy-start.7 = (f32[2,1024,32]{1,2,0:T(8,128)S(1)}, f32[2,1024,32]{1,2,0:T(8,128)}, u32[]{:S(2)}) copy-start(f32[2,1024,32]{1,2,0:T(8,128)} %param.18) | copy-start | bytes 786436
  25.6 8.0 %copy-start.20 = (f32[2,1024]{1,0:T(2,128)S(1)}, f32[2,1024]{1,0:T(2,128)}, u32[]{:S(2)}) copy-start(f32[2,1024]{1,0:T(2,128)} %param.17) | copy-start | bytes 24580
  26.2 10.8 %copy-start.24 = (s32[1,1,16]{2,1,0:T(1,128)}, s32[1,1,16]{2,1,0:T(1,128)S(1)}, u32[]{:S(2)}) copy-start(s32[1,1,16]{2,1,0:T(1,128)S(1)} %get-tuple-element.8) | copy-start | bytes 196
  29.4 0.6 copy-start.8
  30.1 2.8 %copy-start.16 = (s32[1024]{0:T(1024)}, s32[1024]{0:T(1024)S(1)}, u32[]{:S(2)}) copy-start(s32[1024]{0:T(1024)S(1)} %get-tuple-element.48) | copy-start | bytes 12292
  30.1 6.3 %copy-start.14 = (s32[1024]{0:T(1024)}, s32[1024]{0:T(1024)S(1)}, u32[]{:S(2)}) copy-start(s32[1024]{0:T(1024)S(1)} %get-tuple-element.47) | copy-start | bytes 12292
  31.5 4.9 %copy-start.12 = (f32[32,256]{1,0:T(8,128)S(1)}, f32[32,256]{1,0:T(8,128)}, u32[]{:S(2)}) copy-start(f32[32,256]{1,0:T(8,128)} %param.14) | copy-start | bytes 98308
  31.5 4.9 %copy-start.13 = (f32[32,256]{1,0:T(8,128)S(1)}, f32[32,256]{1,0:T(8,128)}, u32[]{:S(2)}) copy-start(f32[32,256]{1,0:T(8,128)} %param.13) | copy-start | bytes 98308
  51.2 15.9 %collective-permute-start.4 = (f32[2,32,32,1]{2,1,3,0:T(8,128)}, f32[2,32,32,1]{2,1,3,0:T(8,128)}, u32[]{:S(2)}, u32[]{:S(2)}) collective-permute-start(f32[2,32,32,1]{2,1,3,0:T(8,128)} %copy.154), channel_id=1, source_target_pairs={{0,1},{1,2},{2,3},{3,4},{4,5},{5,6},{6,7},{7,8},{8,9},{9,10},{10,1... | collective-permute-start | bytes 24584 | tf_op jit(solution)/shard_map/ppermute | solution.py:17
  54.2 14.6 %collective-permute-start.5 = (f32[2,32,32,1]{2,1,3,0:T(8,128)}, f32[2,32,32,1]{2,1,3,0:T(8,128)}, u32[]{:S(2)}, u32[]{:S(2)}) collective-permute-start(f32[2,32,32,1]{2,1,3,0:T(8,128)} %copy.156), channel_id=1, source_target_pairs={{1,0},{2,1},{3,2},{4,3},{5,4},{6,5},{7,6},{8,7},{9,8},{10,9},{11,1... | collective-permute-start | bytes 24584 | tf_op jit(solution)/shard_map/ppermute | solution.py:20
  57.3 14.1 %collective-permute-start.6 = (f32[2,32,1,256]{3,1,2,0:T(8,128)}, f32[2,32,1,256]{3,1,2,0:T(8,128)}, u32[]{:S(2)}, u32[]{:S(2)}) collective-permute-start(f32[2,32,1,256]{3,1,2,0:T(8,128)} %get-tuple-element.15), channel_id=1, source_target_pairs={{0,64},{64,128},{128,192},{1,65},{65,129},{129,193},{2,66},{66,130... | collective-permute-start | bytes 196616 | tf_op jit(solution)/shard_map/ppermute | solution.py:17
  64.0 7.4 %collective-permute-start.7 = (f32[2,32,1,256]{3,1,2,0:T(8,128)}, f32[2,32,1,256]{3,1,2,0:T(8,128)}, u32[]{:S(2)}, u32[]{:S(2)}) collective-permute-start(f32[2,32,1,256]{3,1,2,0:T(8,128)} %get-tuple-element.16), channel_id=1, source_target_pairs={{64,0},{128,64},{192,128},{65,1},{129,65},{193,129},{66,2},{130,66... | collective-permute-start | bytes 196616 | tf_op jit(solution)/shard_map/ppermute | solution.py:20
  76.0 1.3 copy-start
  77.4 4.4 %copy-start.22 = (pred[16]{0:T(512)(128)(4,1)S(1)}, pred[16]{0:T(512)(128)(4,1)}, u32[]{:S(2)}) copy-start(pred[16]{0:T(512)(128)(4,1)} %get-tuple-element.45) | copy-start | bytes 52
  77.4 4.5 %copy-start.25 = (s32[1,1,16]{2,1,0:T(1,128)S(1)}, s32[1,1,16]{2,1,0:T(1,128)}, u32[]{:S(2)}) copy-start(s32[1,1,16]{2,1,0:T(1,128)} %copy-done.24) | copy-start | bytes 196
  77.4 4.5 %copy-start.26 = (s32[16]{0:T(128)S(1)}, s32[16]{0:T(128)}, u32[]{:S(2)}) copy-start(s32[16]{0:T(128)} %gather_fusion.8) | copy-start | bytes 196
  77.5 4.5 %copy-start.10 = (f32[3,5,16]{2,0,1:T(4,128)S(1)}, f32[3,5,16]{2,0,1:T(4,128)}, u32[]{:S(2)}) copy-start(f32[3,5,16]{2,0,1:T(4,128)} %copy_select_fusion.1) | copy-start | bytes 2884
  77.5 4.8 %copy-start.17 = (s32[1024]{0:T(1024)S(1)}, s32[1024]{0:T(1024)}, u32[]{:S(2)}) copy-start(s32[1024]{0:T(1024)} %copy-done.16) | copy-start | bytes 12292
  80.1 4.3 %copy-start.23 = (f32[240]{0:T(256)S(1)}, f32[240]{0:T(256)}, u32[]{:S(2)}) copy-start(f32[240]{0:T(256)} %convert_divide_fusion) | copy-start | bytes 2884
  80.1 25.3 %copy-start.6 = (f32[2,32,256]{2,1,0:T(8,128)S(1)}, f32[2,32,256]{2,1,0:T(8,128)}, u32[]{:S(2)}) copy-start(f32[2,32,256]{2,1,0:T(8,128)} %get-tuple-element.9) | copy-start | bytes 196612
  81.9 15.7 %collective-permute-start.8 = (f32[16,32]{1,0:T(8,128)S(1)}, f32[16,32]{1,0:T(8,128)S(1)}, u32[]{:S(2)}, u32[]{:S(2)}) collective-permute-start(f32[16,32]{1,0:T(8,128)S(1)} %broadcast_select_fusion.1), channel_id=1, source_target_pairs={{0,2},{1,3},{2,4},{3,5},{4,6},{5,7},{6,8},{7,9},{8,10},{9,11},{10,... | collective-permute-start | bytes 6152 | tf_op jit(solution)/shard_map/ppermute | solution.py:27
  82.2 36.7 %copy-start.1 = (f32[2,32,32,256]{3,1,2,0:T(8,128)S(1)}, f32[2,32,32,256]{3,1,2,0:T(8,128)}, u32[]{:S(2)}) copy-start(f32[2,32,32,256]{3,1,2,0:T(8,128)} %copy-done) | copy-start | bytes 6291460
  84.5 13.1 %collective-permute-start.9 = (f32[16,32]{1,0:T(8,128)S(1)}, f32[16,32]{1,0:T(8,128)S(1)}, u32[]{:S(2)}, u32[]{:S(2)}) collective-permute-start(f32[16,32]{1,0:T(8,128)S(1)} %broadcast_select_fusion.1), channel_id=1, source_target_pairs={{0,1},{1,2},{2,3},{3,4},{4,5},{5,6},{6,7},{7,8},{8,9},{9,10},{10,1... | collective-permute-start | bytes 6152 | tf_op jit(solution)/shard_map/ppermute | solution.py:27
  86.6 11.0 %collective-permute-start.10 = (f32[16,32]{1,0:T(8,128)S(1)}, f32[16,32]{1,0:T(8,128)S(1)}, u32[]{:S(2)}, u32[]{:S(2)}) collective-permute-start(f32[16,32]{1,0:T(8,128)S(1)} %broadcast_select_fusion.1), channel_id=1, source_target_pairs={{0,63},{1,0},{2,1},{3,2},{4,3},{5,4},{6,5},{7,6},{8,7},{9,8},{10,9... | collective-permute-start | bytes 6152 | tf_op jit(solution)/shard_map/ppermute | solution.py:27
  91.7 6.7 %collective-permute-start.11 = (f32[16,32]{1,0:T(8,128)S(1)}, f32[16,32]{1,0:T(8,128)S(1)}, u32[]{:S(2)}, u32[]{:S(2)}) collective-permute-start(f32[16,32]{1,0:T(8,128)S(1)} %broadcast_select_fusion.1), channel_id=1, source_target_pairs={{0,62},{1,63},{2,0},{3,1},{4,2},{5,3},{6,4},{7,5},{8,6},{9,7},{10,... | collective-permute-start | bytes 6152 | tf_op jit(solution)/shard_map/ppermute | solution.py:27
  98.4 7.1 %collective-permute-start.12 = (f32[1,5,16,32]{3,2,1,0:T(8,128)S(1)}, f32[1,5,16,32]{3,2,1,0:T(8,128)S(1)}, u32[]{:S(2)}, u32[]{:S(2)}) collective-permute-start(f32[1,5,16,32]{3,2,1,0:T(8,128)S(1)} %bitcast.204), channel_id=1, source_target_pairs={{0,64},{64,128},{128,192},{1,65},{65,129},{129,193},{2,66},{66,130... | collective-permute-start | bytes 30728 | tf_op jit(solution)/shard_map/ppermute | solution.py:17
  104.1 6.6 %collective-permute-start.13 = (f32[1,5,16,32]{3,2,1,0:T(8,128)S(1)}, f32[1,5,16,32]{3,2,1,0:T(8,128)S(1)}, u32[]{:S(2)}, u32[]{:S(2)}) collective-permute-start(f32[1,5,16,32]{3,2,1,0:T(8,128)S(1)} %bitcast.205), channel_id=1, source_target_pairs={{64,0},{128,64},{192,128},{65,1},{129,65},{193,129},{66,2},{130,66... | collective-permute-start | bytes 30728 | tf_op jit(solution)/shard_map/ppermute | solution.py:20
  121.0 1.3 copy-start.2
  122.4 4.4 %copy-start.21 = (pred[16]{0:T(512)(128)(4,1)S(1)}, pred[16]{0:T(512)(128)(4,1)}, u32[]{:S(2)}) copy-start(pred[16]{0:T(512)(128)(4,1)} %get-tuple-element.6) | copy-start | bytes 52
  122.4 4.5 %copy-start.9 = (s32[3,5,16]{2,0,1:T(4,128)S(1)}, s32[3,5,16]{2,0,1:T(4,128)}, u32[]{:S(2)}) copy-start(s32[3,5,16]{2,0,1:T(4,128)} %copy-done.8) | copy-start | bytes 2884
  122.4 4.7 %copy-start.15 = (s32[1024]{0:T(1024)S(1)}, s32[1024]{0:T(1024)}, u32[]{:S(2)}) copy-start(s32[1024]{0:T(1024)} %copy-done.14) | copy-start | bytes 12292
  126.9 12.8 %collective-permute-start.14 = (f32[16,32]{1,0:T(8,128)S(1)}, f32[16,32]{1,0:T(8,128)S(1)}, u32[]{:S(2)}, u32[]{:S(2)}) collective-permute-start(f32[16,32]{1,0:T(8,128)S(1)} %broadcast_select_fusion), channel_id=1, source_target_pairs={{0,2},{1,3},{2,4},{3,5},{4,6},{5,7},{6,8},{7,9},{8,10},{9,11},{10,... | collective-permute-start | bytes 6152 | tf_op jit(solution)/shard_map/ppermute | solution.py:27
  127.1 33.1 %copy-start.3 = (f32[2,32,32,256]{3,1,2,0:T(8,128)S(1)}, f32[2,32,32,256]{3,1,2,0:T(8,128)}, u32[]{:S(2)}) copy-start(f32[2,32,32,256]{3,1,2,0:T(8,128)} %copy-done.2) | copy-start | bytes 6291460
  129.3 10.4 %collective-permute-start.15 = (f32[16,32]{1,0:T(8,128)S(1)}, f32[16,32]{1,0:T(8,128)S(1)}, u32[]{:S(2)}, u32[]{:S(2)}) collective-permute-start(f32[16,32]{1,0:T(8,128)S(1)} %broadcast_select_fusion), channel_id=1, source_target_pairs={{0,1},{1,2},{2,3},{3,4},{4,5},{5,6},{6,7},{7,8},{8,9},{9,10},{10,1... | collective-permute-start | bytes 6152 | tf_op jit(solution)/shard_map/ppermute | solution.py:27
  132.2 7.5 %collective-permute-start.16 = (f32[16,32]{1,0:T(8,128)S(1)}, f32[16,32]{1,0:T(8,128)S(1)}, u32[]{:S(2)}, u32[]{:S(2)}) collective-permute-start(f32[16,32]{1,0:T(8,128)S(1)} %broadcast_select_fusion), channel_id=1, source_target_pairs={{0,63},{1,0},{2,1},{3,2},{4,3},{5,4},{6,5},{7,6},{8,7},{9,8},{10,9... | collective-permute-start | bytes 6152 | tf_op jit(solution)/shard_map/ppermute | solution.py:27
  133.4 7.1 %collective-permute-start.17 = (f32[16,32]{1,0:T(8,128)S(1)}, f32[16,32]{1,0:T(8,128)S(1)}, u32[]{:S(2)}, u32[]{:S(2)}) collective-permute-start(f32[16,32]{1,0:T(8,128)S(1)} %broadcast_select_fusion), channel_id=1, source_target_pairs={{0,62},{1,63},{2,0},{3,1},{4,2},{5,3},{6,4},{7,5},{8,6},{9,7},{10,... | collective-permute-start | bytes 6152 | tf_op jit(solution)/shard_map/ppermute | solution.py:27
  140.5 7.4 %collective-permute-start.18 = (f32[1,5,16,32]{3,2,1,0:T(8,128)S(1)}, f32[1,5,16,32]{3,2,1,0:T(8,128)S(1)}, u32[]{:S(2)}, u32[]{:S(2)}) collective-permute-start(f32[1,5,16,32]{3,2,1,0:T(8,128)S(1)} %bitcast.209), channel_id=1, source_target_pairs={{0,64},{64,128},{128,192},{1,65},{65,129},{129,193},{2,66},{66,130... | collective-permute-start | bytes 30728 | tf_op jit(solution)/shard_map/ppermute | solution.py:17
  146.3 5.6 %collective-permute-start.19 = (f32[1,5,16,32]{3,2,1,0:T(8,128)S(1)}, f32[1,5,16,32]{3,2,1,0:T(8,128)S(1)}, u32[]{:S(2)}, u32[]{:S(2)}) collective-permute-start(f32[1,5,16,32]{3,2,1,0:T(8,128)S(1)} %bitcast.210), channel_id=1, source_target_pairs={{64,0},{128,64},{192,128},{65,1},{129,65},{193,129},{66,2},{130,66... | collective-permute-start | bytes 30728 | tf_op jit(solution)/shard_map/ppermute | solution.py:20
where the time goes:
time: 168 us; the launch traced here: 165 us
  starting transfers between devices  60.5 us (36%)
  local copies, waits for them, and re-layouts  56.2 us (33%)
  other arithmetic  29.6 us (18%)
  waiting for transfers between devices  10.7 us (6%)
  matrix products  6.73 us (4%)
    ppermute x6, starting transfers between devices, extended(): lax.ppermute(lax.slice_in_dim(block, block.shape[dim] - width, None, axis...  28.5 us
    ppermute x8, starting transfers between devices, from_behind(): lax.ppermute(x, axis, [(i, (i + by) % length) for i in range(length)])  23.5 us
    ppermute x6, waiting for transfers between devices, extended(): lax.ppermute(lax.slice_in_dim(block, 0, width, axis=dim), axis, backward)  9.3 us
    scatter x2, local copies, waits for them, and re-layouts, slot_table(): table = table.at[tile_of * slot_count + rank].set(order, mode='drop')  8.84 us
    ppermute x6, starting transfers between devices, extended(): lax.ppermute(lax.slice_in_dim(block, 0, width, axis=dim), axis, backward)  8.51 us
    unnamed x65, local copies, waits for them, and re-layouts  7.39 us
    another operation x6, other arithmetic, transform_of(): factor = jnp.linalg.cholesky(system)  7.22 us
    add x1, other arithmetic, combine_terms(): out + diff_rate * (west_side + east_side + south_side + north_side - 4.0...  6.42 us
  transfers between devices with their start and end apart: 20, of which 4 were waited for; matrix products, arithmetic and copies ran while one was open for 23% of the time, Pallas kernels for 0%

commit v1 on v0

v1 whole, which is shorter than its diff:
```python
import jax
import jax.numpy as jnp
from jax import lax
from jax.experimental import pallas as pl
from jax.experimental.pallas import tpu as pltpu
from jax.sharding import PartitionSpec as P

MESH = pl.DeviceIdType.MESH
HI = lax.Precision.HIGHEST
F, M, R, C = 2, 32, 32, 256
H = 128
SLOTS = 16
BATCHES = 2
REACH = tuple((di, dj) for di in (-1, 0, 1) for dj in range(-2, 3) if (di, dj) != (0, 0))
ROWS, COLS, CORNER, CROWS, CCOLS = 0, 4, 8, 12, 14
CHANNELS = 16


def iota(shape, axis):
    return lax.broadcasted_iota(jnp.int32, shape, axis)


def dot(a, b):
    return lax.dot_general(a, b, (((1,), (0,)), ((), ())), precision=HI, preferred_element_type=jnp.float32)


def eliminate(system):
    parts = [system[8 * g : 8 * g + 8] for g in range(4)]
    sub = iota((8, H), 0)
    for k in range(M):
        own, at = divmod(k, 8)
        columns = [jnp.broadcast_to(part[:, k : k + 1], (8, H)) for part in parts]
        pivot = jnp.broadcast_to(columns[own][at : at + 1, :], (8, H))
        row = jnp.broadcast_to(parts[own][at : at + 1, :], (8, H)) * (1.0 / pivot)
        new = [part - column * row for part, column in zip(parts, columns)]
        new[own] = jnp.where(sub == at, row, new[own])
        parts = new
    return jnp.concatenate(parts, axis=0)


def forecast_kernel(
    ens, cx_in, cy_in, diff_in, cell_in, value_in, noise_in, var_in,
    x_out, e_out,
    halves, q, x1, x2, own_w, own_e, far_w, far_e, next_w, next_e, corner_s, corner_r, crow_s, crow_r, ccol_s, ccol_r,
    coef, cx, cy, diff, cell, cell16, value, noise, var, id_v, id_s, vn, sw, msg, got,
    in_sem, out_sem, p1_send, p1_recv, p2_send, p2_recv,
):
    la, lo = lax.axis_size("lat"), lax.axis_size("lon")
    me_i, me_j = lax.axis_index("lat"), lax.axis_index("lon")

    def at(di, dj):
        return (lax.rem(me_i + (di + la), la), lax.rem(me_j + (dj + lo), lo))

    barrier = pltpu.get_barrier_semaphore()
    for di, dj in REACH:
        pl.semaphore_signal(barrier, inc=1, device_id=at(di, dj), device_id_type=MESH)

    def load(src, dst, sem):
        copy = pltpu.make_async_copy(src, dst, in_sem.at[sem])
        copy.start()
        return copy

    ens_copies = [
        [load(ens.at[f, :, pl.ds(h * H, H)], halves.at[h, f], 2 * f + h) for h in range(2)] for f in range(F)
    ]
    c_copies = [load(cx_in, cx, 4), load(cy_in, cy, 5), load(diff_in, diff, 6)]
    o_copies = [load(cell_in, cell, 7), load(value_in, value, 8), load(var_in, var, 9)]
    n_copy = load(noise_in, noise, 10)

    lane = iota((M, H), 1)
    lane8 = iota((8, H), 1)
    started = []

    def send(channel, src, dst, target):
        copy = pltpu.make_async_remote_copy(
            src_ref=src, dst_ref=dst, send_sem=p1_send.at[channel], recv_sem=p1_recv.at[channel],
            device_id=target, device_id_type=MESH,
        )
        copy.start()
        started.append(copy)
        return copy

    for copy in c_copies:
        copy.wait()
    cxv, cyv = cx[...], cy[...]
    for side, row in ((0, R - 1), (1, 0)):
        crow_s[side, 0:1, :] = cxv[row : row + 1, :]
        crow_s[side, 1:2, :] = cyv[row : row + 1, :]
    spot = (lax.shift_right_logical(lane, 1) == iota((R, H), 0)) & (lane < 2 * R)
    for side, col in ((0, C - 1), (1, 0)):
        for n, source in enumerate((cxv, cyv)):
            spread = jnp.where(spot, jnp.broadcast_to(source[:, col : col + 1], (R, H)), 0.0)
            ccol_s[side, n : n + 1, :] = jnp.sum(spread, axis=0, keepdims=True)

    def pack(f):
        for copy in ens_copies[f]:
            copy.wait()
        def body(r, carry):
            west, east = carry
            c0 = halves[0, f, pl.ds(r, M, stride=R), :]
            c1 = halves[1, f, pl.ds(r, M, stride=R), :]
            q[f, r + 2, :, 0:H] = c0
            q[f, r + 2, :, H:C] = c1
            here = lax.shift_right_logical(lane, 1) == r
            west = jnp.where(here, pltpu.roll(c0, 2 * r, 1), west)
            east = jnp.where(here, pltpu.roll(c1, lax.rem(2 * r + 2, H), 1), east)
            return west, east

        zero = jnp.zeros((M, H), jnp.float32)
        west, east = lax.fori_loop(0, R, body, (zero, zero), unroll=8)
        own_w[f] = west
        own_e[f] = east

    def send_field(f):
        return [
            send(ROWS + 2 * f, q.at[f, pl.ds(R, 2)], q.at[f, pl.ds(0, 2)], at(1, 0)),
            send(ROWS + 2 * f + 1, q.at[f, pl.ds(2, 2)], q.at[f, pl.ds(R + 2, 2)], at(-1, 0)),
            send(COLS + 2 * f, own_e.at[f], far_w.at[f], at(0, 1)),
            send(COLS + 2 * f + 1, own_w.at[f], far_e.at[f], at(0, -1)),
        ]

    pack(0)
    pl.semaphore_wait(barrier, len(REACH))
    field_copies = [send_field(0)]
    halo_copies = [
        send(CROWS, crow_s.at[0], crow_r.at[0], at(1, 0)),
        send(CROWS + 1, crow_s.at[1], crow_r.at[1], at(-1, 0)),
        send(CCOLS, ccol_s.at[0], ccol_r.at[0], at(0, 1)),
        send(CCOLS + 1, ccol_s.at[1], ccol_r.at[1], at(0, -1)),
    ]
    pack(1)
    fill = jnp.zeros((H - F * M, H), jnp.float32)
    turned_w = jnp.concatenate([own_w[0], own_w[1], fill], axis=0).T
    turned_e = jnp.concatenate([own_e[0], own_e[1], fill], axis=0).T
    corner_s[0] = turned_e[2 * R - 8 : 2 * R]
    corner_s[1] = turned_w[2 * R - 8 : 2 * R]
    corner_s[2] = turned_e[0:8]
    corner_s[3] = turned_w[0:8]
    for n, target in enumerate(((1, 1), (1, -1), (-1, 1), (-1, -1))):
        halo_copies.append(send(CORNER + n, corner_s.at[n], corner_r.at[n], at(*target)))
    field_copies.append(send_field(1))

    for copy in o_copies:
        copy.wait()
    count = cell.shape[1]
    chunks = count // H
    wide = lo * C
    shift = wide.bit_length() - 1
    n_rows = BATCHES * chunks
    for ch in range(chunks):
        cell16[BATCHES * ch : BATCHES * (ch + 1), :] = cell[:, ch * H : (ch + 1) * H]
    cells = cell16[...]
    l_row = lax.shift_right_logical(cells, shift) - me_i * R
    l_col = (cells & (wide - 1)) - me_j * C
    mine = (l_row >= 0) & (l_row < R) & (l_col >= 0) & (l_col < C)
    mask = jnp.where(mine, 1.0, 0.0)
    before = jnp.where(iota((H, H), 0) < iota((H, H), 1), 1.0, 0.0)
    ii, jj = iota((n_rows, n_rows), 0), iota((n_rows, n_rows), 1)
    rows_before = jnp.where((lax.rem(ii, BATCHES) == lax.rem(jj, BATCHES)) & (jj < ii), 1.0, 0.0)
    totals = jnp.broadcast_to(jnp.sum(mask, axis=1, keepdims=True), (n_rows, H))
    rank = dot(mask, before) + dot(rows_before, totals)
    rank = jnp.where(mine, rank, -1.0).astype(jnp.int32)
    order = lax.shift_right_logical(iota((n_rows, H), 0), 1) * H + iota((n_rows, H), 1)
    code = jnp.where(mine, (order * R + l_row) * C + l_col, 0).astype(jnp.float32)
    slot = iota((SLOTS, H), 0)
    slot_lane = iota((SLOTS, H), 1)
    columns = []
    for b in range(BATCHES):
        acc = [jnp.zeros((SLOTS, H), jnp.float32) for _ in range(3)]
        for ch in range(chunks):
            at_row = BATCHES * ch + b
            here = jnp.broadcast_to(rank[at_row : at_row + 1, :], (SLOTS, H)) == slot
            cut = slice(ch * H, (ch + 1) * H)
            for n, source in enumerate((code[at_row : at_row + 1, :], value[b : b + 1, cut], var[b : b + 1, cut])):
                acc[n] = jnp.where(here, jnp.broadcast_to(source, (SLOTS, H)), acc[n])
        sums = [jnp.broadcast_to(jnp.sum(a, axis=1, keepdims=True), (SLOTS, H)) for a in acc]
        id_v[b * SLOTS : (b + 1) * SLOTS, :] = sums[0].astype(jnp.int32)
        there = sums[2] > 0.0
        sw[b] = jnp.where(there, jnp.sqrt(1.0 / jnp.where(there, sums[2], 1.0)), 0.0)
        columns.append(sums[1])
    id_copy = load(id_v, id_s, 11)

    def parts_of(x, y):
        return jnp.maximum(x, 0.0), -jnp.minimum(x, 0.0), jnp.maximum(y, 0.0), -jnp.minimum(y, 0.0)

    rates = [diff[f] for f in range(F)]
    low_edge, high_edge = me_i == 0, me_i == la - 1

    def centre_of(p, k):
        return 1.0 - p[0] - p[1] - p[2] - p[3] - 4.0 * k

    own_parts = parts_of(cxv, cyv)
    row_id = iota((R, C), 0)

    def set_coef(f, first, values):
        for n in range(5):
            for h in range(2):
                v = values[n][:, h * H : (h + 1) * H]
                coef[f, n, h, first : first + max(8, v.shape[0]), :] = jnp.broadcast_to(v, (max(8, v.shape[0]), H))

    for f in range(F):
        south = jnp.where((row_id == 0) & low_edge, 0.0, own_parts[2] + rates[f])
        north = jnp.where((row_id == R - 1) & high_edge, 0.0, own_parts[3] + rates[f])
        set_coef(f, 8, [centre_of(own_parts, rates[f]), own_parts[0] + rates[f], own_parts[1] + rates[f], south, north])

    id_copy.wait()
    n_copy.wait()
    ids = [[id_s[b * SLOTS + s, 0] for s in range(SLOTS)] for b in range(BATCHES)]
    slot_m = iota((SLOTS, M), 0)
    move = jnp.where(iota((M, H), 1) == iota((M, H), 0) + M, 1.0, 0.0)
    middle = (slot_lane >= M) & (slot_lane < 2 * M)
    for b in range(BATCHES):
        rows = jnp.zeros((SLOTS, M), jnp.float32)
        for s in range(SLOTS):
            one = noise[b, pl.ds(lax.shift_right_logical(ids[b][s], 13) & (count - 1), 1), :]
            rows = jnp.where(slot_m == s, jnp.broadcast_to(one, (SLOTS, M)), rows)
        vn[b] = jnp.where(middle, columns[b] + dot(rows, move), 0.0)

    for copy in halo_copies:
        copy.wait_recv()
    halo_rows = [parts_of(crow_r[side, 0:1, :], crow_r[side, 1:2, :]) for side in range(2)]
    for f in range(F):
        for side, first in ((0, 0), (1, 8 + R)):
            p = halo_rows[side]
            values = [centre_of(p, rates[f])] + [part + rates[f] for part in p]
            set_coef(f, first, values)
    corners = jnp.concatenate([corner_r[n] for n in range(4)] + [jnp.zeros((H - 32, H), jnp.float32)], axis=0).T

    def halo_columns(f):
        for copy in field_copies[f][2:]:
            copy.wait_recv()
        corner = [
            jnp.broadcast_to(corners[f * M : (f + 1) * M, n : n + 1], (M, H)) for n in (7, 14, 17, 24)
        ]
        west = far_w[f]
        west = jnp.where(lane == H - 1, corner[0], jnp.where(lane == 2 * R + 1, corner[2], west))
        east = far_e[f]
        east = jnp.where(lane == H - 2, corner[1], jnp.where(lane == 2 * R, corner[3], east))
        far_w[f] = west
        far_e[f] = east
        lane_row = iota((1, H), 1)
        for side in range(2):
            p = parts_of(ccol_r[side, 0:1, :], ccol_r[side, 1:2, :])
            south = jnp.where((lane_row < 2) & low_edge, 0.0, p[2] + rates[f])
            north = jnp.where((lane_row >= 2 * R - 2) & high_edge, 0.0, p[3] + rates[f])
            rate = (centre_of(p, rates[f]), p[0] + rates[f], p[1] + rates[f], south, north)
            if side == 0:
                c, w, e = west, pltpu.roll(west, 1, 1), pltpu.roll(own_w[f], 1, 1)
            else:
                c, w, e = east, pltpu.roll(own_e[f], H - 1, 1), pltpu.roll(east, H - 1, 1)
            out = rate[0] * c + rate[1] * w + rate[2] * e
            out = out + rate[3] * pltpu.roll(c, 2, 1) + rate[4] * pltpu.roll(c, H - 2, 1)
            out = jnp.where(lane < 2 * R, out, 0.0)
            if side == 0:
                next_w[f] = out
            else:
                next_e[f] = out

    def row_step(src, dst, f, r, src_at, dst_at, far_west, far_east):
        turn = (H - 1 - 2 * r) & (H - 1)
        hw, he = pltpu.roll(far_west, turn, 1), pltpu.roll(far_east, turn, 1)
        c0, c1 = src[f, r + src_at, :, 0:H], src[f, r + src_at, :, H:C]
        w0, w1 = pltpu.roll(c0, 1, 1), pltpu.roll(c1, 1, 1)
        e0, e1 = pltpu.roll(c0, H - 1, 1), pltpu.roll(c1, H - 1, 1)
        first, last = lane == 0, lane == H - 1
        w0, w1 = jnp.where(first, hw, w0), jnp.where(first, w0, w1)
        e0, e1 = jnp.where(last, e1, e0), jnp.where(last, he, e1)
        for h, (c, w, e) in enumerate(((c0, w0, e0), (c1, w1, e1))):
            cut = slice(h * H, (h + 1) * H)
            rate = [coef[f, n, h, pl.ds(r + 8, 1), :] for n in range(5)]
            out = rate[0] * c + rate[1] * w + rate[2] * e
            out = out + rate[3] * src[f, r + src_at - 1, :, cut] + rate[4] * src[f, r + src_at + 1, :, cut]
            dst[f, r + dst_at, :, cut] = out

    def step_one(f, r):
        row_step(q, x1, f, r, 2, 1, far_w[f], far_e[f])

    def step_two(f, r):
        row_step(x1, x2, f, r, 1, 0, next_w[f], next_e[f])

    def rows_of(step, f, begin, end):
        def body(r, carry):
            step(f, r)
            return carry

        lax.fori_loop(begin, end, body, 0, unroll=2)

    def forecast(f):
        halo_columns(f)
        rows_of(step_one, f, 1, R - 1)
        rows_of(step_two, f, 2, R - 2)
        for copy in field_copies[f][:2]:
            copy.wait_recv()
        for r in (-1, 0, R - 1, R):
            step_one(f, r)
        for r in (0, 1, R - 2, R - 1):
            step_two(f, r)
        copy = pltpu.make_async_copy(x2.at[f], x_out.at[f], out_sem.at[f])
        copy.start()
        return copy

    def observe(b):
        f = b % F
        seen = jnp.zeros((M, H), jnp.float32)
        for s in range(SLOTS):
            code_s = ids[b][s]
            row = x2[f, lax.shift_right_logical(code_s, 8) & (R - 1)]
            col = code_s & (C - 1)
            picked = jnp.where(lane == col, row[:, 0:H], 0.0) + jnp.where(lane + H == col, row[:, H:C], 0.0)
            seen = jnp.where(lane == s, jnp.broadcast_to(jnp.sum(picked, axis=1, keepdims=True), (M, H)), seen)
        mean = jnp.sum(seen, axis=0, keepdims=True) * (1.0 / M)
        stacked = jnp.concatenate([seen - mean, seen, jnp.zeros((H - 2 * M, H), jnp.float32)], axis=0)
        return stacked.T[0:SLOTS]

    def tell(b, z):
        signed = jnp.where(slot_lane < M, z, -z)
        r = sw[b] * (vn[b] + signed)
        r = jnp.where(slot_lane < 2 * M, r, 0.0)
        packed = r[0:8] + pltpu.roll(r[8:16], 2 * M, 1)
        msg[b] = packed
        got[b, 14] = packed
        got[b, 15] = jnp.zeros((8, H), jnp.float32)
        copies = []
        for n, (di, dj) in enumerate(REACH):
            copy = pltpu.make_async_remote_copy(
                src_ref=msg.at[b], dst_ref=got.at[b, n], send_sem=p2_send.at[b, n], recv_sem=p2_recv.at[b, n],
                device_id=at(-di, -dj), device_id_type=MESH,
            )
            copy.start()
            copies.append(copy)
        started.extend(copies)
        return copies

    lower = iota((8, H), 0)

    def transform(b, copies):
        for copy in copies:
            copy.wait_recv()
        stack = got[b].reshape(16 * 8, H)
        place = iota((16 * 8, H), 0)
        keep = jnp.where(low_edge & (place < 5 * 8), 0.0, 1.0)
        keep = jnp.where(high_edge & (place >= 9 * 8) & (place < 14 * 8), 0.0, keep)
        stack = stack * keep
        turned = stack.T
        gram = dot(jnp.concatenate([turned[0:M], turned[2 * M : 3 * M]], axis=0), stack)
        both = gram[0:M] + pltpu.roll(gram[M : 2 * M], 2 * M, 1)
        system = jnp.where(lane < 2 * M, both, 0.0) + jnp.where(lane == iota((M, H), 0), M - 1.0, 0.0)
        return eliminate(system)

    def centered_rows(solved):
        w = jnp.where(lane < M, pltpu.roll(solved, H - M, 1), 0.0)
        return w - jnp.sum(w, axis=0, keepdims=True) * (1.0 / M)

    outs = [forecast(0)]
    z0 = observe(0)
    copies0 = tell(0, z0)
    outs.append(forecast(1))
    z1 = observe(1)
    solved0 = transform(0, copies0)
    w0 = jnp.where(lane < M, pltpu.roll(solved0, H - M, 1), 0.0)
    w0_mean = jnp.sum(w0, axis=1, keepdims=True) * (1.0 / M)
    both0 = jnp.where(lane < M, w0 - w0_mean, jnp.where(lane < 2 * M, solved0, 0.0))
    z1 = z1 + dot(z1[:, 0:M], both0)
    copies1 = tell(1, z1)
    c0 = centered_rows(solved0)
    solved1 = transform(1, copies1)
    c1 = centered_rows(solved1)
    e_out[...] = c0 + c1 + dot(c0[:, 0:M], c1)

    for copy in started:
        copy.wait_send()
    for copy in outs:
        copy.wait()


def analysis_kernel(e_ref, x_in, out, x, y, in_sem, out_sem):
    groups = [(f, r) for f in range(F) for r in range(0, R, 8)]
    loads = []
    for n, (f, r) in enumerate(groups):
        copy = pltpu.make_async_copy(x_in.at[f, pl.ds(r, 8)], x.at[f, pl.ds(r, 8)], in_sem.at[n])
        copy.start()
        loads.append(copy)
    e = jnp.concatenate([e_ref[...], jnp.zeros((H - M, H), jnp.float32)], axis=0).T[0:M, 0:M]
    e_hi = e.astype(jnp.bfloat16)
    e_lo = (e - e_hi.astype(jnp.float32)).astype(jnp.bfloat16)
    left = jnp.concatenate([e_hi, e_hi, e_lo], axis=1)
    stores = []
    for n, (f, r) in enumerate(groups):
        loads[n].wait()
        for row in range(r, r + 8):
            v = x[f, row]
            hi = v.astype(jnp.bfloat16)
            low = (v - hi.astype(jnp.float32)).astype(jnp.bfloat16)
            right = jnp.concatenate([hi, low, hi], axis=0)
            add = lax.dot_general(left, right, (((1,), (0,)), ((), ())), preferred_element_type=jnp.float32)
            y[f, row] = v + add
        for row in range(r, r + 8):
            copy = pltpu.make_async_copy(y.at[f, row], out.at[f, :, row, :], out_sem.at[f, row])
            copy.start()
            stores.append(copy)
    for copy in stores:
        copy.wait()


def local(ensemble, courant_x, courant_y, diffusion, obs_cell, obs_value, obs_noise, obs_var, loc_mask):
    any_space = pl.BlockSpec(memory_space=pl.ANY)
    f32 = jnp.float32
    count = obs_cell.shape[1]
    vmem = pltpu.VMEM
    dma = pltpu.SemaphoreType.DMA
    forecast, combined = pl.pallas_call(
        forecast_kernel,
        out_shape=(jax.ShapeDtypeStruct((F, R, M, C), f32), jax.ShapeDtypeStruct((M, H), f32)),
        in_specs=[any_space] * 8,
        out_specs=(any_space, pl.BlockSpec(memory_space=pltpu.VMEM)),
        scratch_shapes=[
            vmem((2, F, M * R, H), f32),
            vmem((F, R + 4, M, C), f32),
            vmem((F, R + 2, M, C), f32),
            vmem((F, R, M, C), f32),
            vmem((F, M, H), f32),
            vmem((F, M, H), f32),
            vmem((F, M, H), f32),
            vmem((F, M, H), f32),
            vmem((F, M, H), f32),
            vmem((F, M, H), f32),
            vmem((4, 8, H), f32),
            vmem((4, 8, H), f32),
            vmem((2, 8, C), f32),
            vmem((2, 8, C), f32),
            vmem((2, 8, H), f32),
            vmem((2, 8, H), f32),
            vmem((F, 5, 2, R + 16, H), f32),
            vmem((R, C), f32),
            vmem((R, C), f32),
            pltpu.SMEM((F,), f32),
            vmem((BATCHES, count), jnp.int32),
            vmem((BATCHES * count // H, H), jnp.int32),
            vmem((BATCHES, count), f32),
            vmem((BATCHES, count, M), f32),
            vmem((BATCHES, count), f32),
            vmem((BATCHES * SLOTS, H), jnp.int32),
            pltpu.SMEM((BATCHES * SLOTS, H), jnp.int32),
            vmem((BATCHES, SLOTS, H), f32),
            vmem((BATCHES, SLOTS, H), f32),
            vmem((BATCHES, 8, H), f32),
            vmem((BATCHES, 16, 8, H), f32),
            dma((12,)),
            dma((F,)),
            dma((CHANNELS,)),
            dma((CHANNELS,)),
            dma((BATCHES, len(REACH))),
            dma((BATCHES, len(REACH))),
        ],
        compiler_params=pltpu.CompilerParams(
            collective_id=0, has_side_effects=True, vmem_limit_bytes=40 * 1024 * 1024
        ),
        name="forecast_and_transform",
    )(ensemble.reshape(F, M * R, C), courant_x, courant_y, diffusion, obs_cell, obs_value, obs_noise, obs_var)
    return pl.pallas_call(
        analysis_kernel,
        out_shape=jax.ShapeDtypeStruct((F, M, R, C), f32),
        in_specs=[pl.BlockSpec(memory_space=pltpu.VMEM), any_space],
        out_specs=any_space,
        scratch_shapes=[
            vmem((F, R, M, C), f32),
            vmem((F, R, M, C), f32),
            dma((F * R // 8,)),
            dma((F, R)),
        ],
        compiler_params=pltpu.CompilerParams(vmem_limit_bytes=40 * 1024 * 1024),
        name="analysis",
    )(combined, forecast)


def solution(mesh):
    in_specs = (
        P(None, None, "lat", "lon"),
        P("lat", "lon"),
        P("lat", "lon"),
        P(),
        P(),
        P(),
        P(),
        P(),
        P("lat", "lon", None, None),
    )
    out_specs = P(None, None, "lat", "lon")
    return jax.shard_map(local, mesh=mesh, in_specs=in_specs, out_specs=out_specs, check_vma=False)
```

time: 168 us -> 56.4 us (0.34); the launches traced: 165 us -> 56 us
  starting transfers between devices: 60.5 us -> 0 us
  local copies, waits for them, and re-layouts: 56.2 us -> 7.12 us
  Pallas kernels: 0 us -> 48.9 us
  other arithmetic: 29.6 us -> 0 us
  waiting for transfers between devices: 10.7 us -> 0 us
  matrix products: 6.73 us -> 0 us
    ppermute x20 -> x0, starting transfers between devices: 60.5 us -> none  [the longest x6 28.5 us: extended(): lax.ppermute(lax.slice_in_dim(block, block.shape[dim] - width, None, axis...]
    pallas_call x0 -> x2, Pallas kernels: none -> 48.9 us  [the longest x1 45.5 us: local(): pl.pallas_call(forecast_kernel, out_shape=(jax.ShapeDtypeStruct((F, R, M,...]
    gather x18 -> x0, local copies, waits for them, and re-layouts: 17.2 us -> none  [the longest x2 3.37 us: local(): priors = ensemble[observed_field][:, local_row, local_col].T]
    another operation x10 -> x0, other arithmetic: 13.3 us -> none  [the longest x6 7.22 us: transform_of(): factor = jnp.linalg.cholesky(system)]
    ppermute x20 -> x0, waiting for transfers between devices: 10.7 us -> none  [the longest x6 9.3 us: extended(): lax.ppermute(lax.slice_in_dim(block, 0, width, axis=dim), axis, backward)]
    scatter x2 -> x0, local copies, waits for them, and re-layouts: 8.84 us -> none  [slot_table(): table = table.at[tile_of * slot_count + rank].set(order, mode='drop')]
    ppermute x4 -> x0, local copies, waits for them, and re-layouts: 6.99 us -> none  [the longest x2 4.4 us: extended(): lax.ppermute(lax.slice_in_dim(block, 0, width, axis=dim), axis, backward)]
    slice x10 -> x0, local copies, waits for them, and re-layouts: 6.77 us -> none  [the longest x5 5.42 us: extended(): lax.slice_in_dim(block, block.shape[dim] - width, None, axis=dim)]
  transfers between devices with their start and end apart: 20 -> 0, of which waited for: 4 -> 0; matrix products, arithmetic and copies ran while one was open for 23% -> 0% of each run, Pallas kernels for 0% -> 0%
where the time goes in v1:
time: 56.4 us; the launch traced here: 56 us
  Pallas kernels  48.9 us (87%)
  local copies, waits for them, and re-layouts  7.12 us (13%)
    pallas_call x1, Pallas kernels, local(): pl.pallas_call(forecast_kernel, out_shape=(jax.ShapeDtypeStruct((F, R, M,...  45.5 us
    unnamed x15, local copies, waits for them, and re-layouts  7.12 us
    pallas_call x1, Pallas kernels, local(): pl.pallas_call(analysis_kernel, out_shape=jax.ShapeDtypeStruct((F, M, R,...  3.38 us

profile of v1, /device:TPU:1, one launch (start us, length us, event | category | flops | bytes accessed | tf_op | source)
XLA Modules:
  0.0 56.0 jit_solution(13811738049731418926)
XLA Ops:
  0.0 1.3 %copy.9.noise_in = f32[2,1024,32]{2,1,0:T(8,128)S(1)} copy(f32[2,1024,32]{1,2,0:T(8,128)} %param.15) | data formatting | bytes 524288 | tf_op args[6]
  1.3 0.0 copy-start
  1.3 1.6 %copy-done = f32[2,32,32,256]{3,2,1,0:T(8,128)S(1)} copy-done((f32[2,32,32,256]{3,2,1,0:T(8,128)S(1)}, f32[2,32,32,256]{3,2,1,0:T(8,128)}, u32[]{:S(2)}) %copy-start) | copy-done | bytes 2097176
  2.9 0.0 copy-start.1
  2.9 0.8 %copy-done.1 = f32[32,256]{1,0:T(8,128)S(1)} copy-done((f32[32,256]{1,0:T(8,128)S(1)}, f32[32,256]{1,0:T(8,128)}, u32[]{:S(2)}) %copy-start.1) | copy-done | bytes 32792
  3.6 0.0 copy-start.2
  3.6 0.8 %copy-done.2 = f32[32,256]{1,0:T(8,128)S(1)} copy-done((f32[32,256]{1,0:T(8,128)S(1)}, f32[32,256]{1,0:T(8,128)}, u32[]{:S(2)}) %copy-start.2) | copy-done | bytes 32792
  4.4 0.0 copy-start.3
  4.4 0.7 %copy-done.3 = s32[2,1024]{1,0:T(2,128)S(1)} copy-done((s32[2,1024]{1,0:T(2,128)S(1)}, s32[2,1024]{1,0:T(2,128)}, u32[]{:S(2)}) %copy-start.3) | copy-done | bytes 8216
  5.1 0.0 copy-start.4
  5.1 0.7 %copy-done.4 = f32[2,1024]{1,0:T(2,128)S(1)} copy-done((f32[2,1024]{1,0:T(2,128)S(1)}, f32[2,1024]{1,0:T(2,128)}, u32[]{:S(2)}) %copy-start.4) | copy-done | bytes 8216
  5.8 0.0 copy-start.5
  5.8 0.7 %copy-done.5 = f32[2,1024]{1,0:T(2,128)S(1)} copy-done((f32[2,1024]{1,0:T(2,128)S(1)}, f32[2,1024]{1,0:T(2,128)}, u32[]{:S(2)}) %copy-start.5) | copy-done | bytes 8216
  6.5 0.0 copy-start.6
  6.5 0.7 %copy-done.6 = f32[2]{0:T(128)S(1)} copy-done((f32[2]{0:T(128)S(1)}, f32[2]{0:T(128)}, u32[]{:S(2)}) %copy-start.6) | copy-done | bytes 32
  7.1 45.5 %forecast_and_transform.1 = (f32[2,32,32,256]{3,2,1,0:T(8,128)S(1)}, f32[32,128]{1,0:T(8,128)S(1)}) custom-call(f32[2,1024,256]{2,1,0:T(8,128)S(1)} %bitcast.1, f32[32,256]{1,0:T(8,128)S(1)} %copy-done.1, f32[32,256]{1,0:T(8,128)S(1)} %copy-done.2, f32[2]{0:T(128)S(1)} %copy-done.6, s32[2,1024]{1,0:T(2,128)S(1)} %copy-done.3, f32[2,1024]{1,0:T(2,128)S(1)} %copy-done.4, ...), custom_call_target="tpu_custom_call" | custom-call | tf_op jit(solution)/shard_map/forecast_and_transform/pallas_call | solution.py:411
  52.7 3.4 %analysis.1 = f32[2,32,32,256]{3,2,1,0:T(8,128)} custom-call(f32[32,128]{1,0:T(8,128)S(1)} %get-tuple-element.7.e_ref, f32[2,32,32,256]{3,2,1,0:T(8,128)S(1)} %get-tuple-element.8.x_in), custom_call_target="tpu_custom_call" | custom-call | tf_op jit(solution)/shard_map/analysis/pallas_call | solution.py:460
Async XLA Ops:
  1.3 1.6 %copy-start = (f32[2,32,32,256]{3,2,1,0:T(8,128)S(1)}, f32[2,32,32,256]{3,2,1,0:T(8,128)}, u32[]{:S(2)}) copy-start(f32[2,32,32,256]{3,2,1,0:T(8,128)} %param.9) | copy-start | bytes 6291460
  2.9 0.8 %copy-start.1 = (f32[32,256]{1,0:T(8,128)S(1)}, f32[32,256]{1,0:T(8,128)}, u32[]{:S(2)}) copy-start(f32[32,256]{1,0:T(8,128)} %cx_in.1) | copy-start | bytes 98308
  3.6 0.8 %copy-start.2 = (f32[32,256]{1,0:T(8,128)S(1)}, f32[32,256]{1,0:T(8,128)}, u32[]{:S(2)}) copy-start(f32[32,256]{1,0:T(8,128)} %cy_in.1) | copy-start | bytes 98308
  4.4 0.7 %copy-start.3 = (s32[2,1024]{1,0:T(2,128)S(1)}, s32[2,1024]{1,0:T(2,128)}, u32[]{:S(2)}) copy-start(s32[2,1024]{1,0:T(2,128)} %cell_in.1) | copy-start | bytes 24580
  5.1 0.7 %copy-start.4 = (f32[2,1024]{1,0:T(2,128)S(1)}, f32[2,1024]{1,0:T(2,128)}, u32[]{:S(2)}) copy-start(f32[2,1024]{1,0:T(2,128)} %value_in.1) | copy-start | bytes 24580
  5.8 0.7 %copy-start.5 = (f32[2,1024]{1,0:T(2,128)S(1)}, f32[2,1024]{1,0:T(2,128)}, u32[]{:S(2)}) copy-start(f32[2,1024]{1,0:T(2,128)} %var_in.1) | copy-start | bytes 24580
  6.5 0.7 %copy-start.6 = (f32[2]{0:T(128)S(1)}, f32[2]{0:T(128)}, u32[]{:S(2)}) copy-start(f32[2]{0:T(128)} %diff_in.1) | copy-start | bytes 28

commit v2 on v1

--- a/solution.py
+++ b/solution.py
@@ -27,13 +27,30 @@
 def eliminate(system):
     parts = [system[8 * g : 8 * g + 8] for g in range(4)]
     sub = iota((8, H), 0)
-    for k in range(M):
-        own, at = divmod(k, 8)
-        columns = [jnp.broadcast_to(part[:, k : k + 1], (8, H)) for part in parts]
-        pivot = jnp.broadcast_to(columns[own][at : at + 1, :], (8, H))
-        row = jnp.broadcast_to(parts[own][at : at + 1, :], (8, H)) * (1.0 / pivot)
-        new = [part - column * row for part, column in zip(parts, columns)]
-        new[own] = jnp.where(sub == at, row, new[own])
+    for own in range(4):
+        lanes = range(8 * own, 8 * own + 8)
+        columns = [[jnp.broadcast_to(part[:, k : k + 1], (8, H)) for part in parts] for k in lanes]
+        pivots = [[jnp.broadcast_to(columns[j][own][i : i + 1], (8, H)) for j in range(8)] for i in range(8)]
+        rows = [jnp.broadcast_to(parts[own][i : i + 1], (8, H)) for i in range(8)]
+        for p in range(8):
+            inverse = 1.0 / pivots[p][p]
+            rows[p] = rows[p] * inverse
+            for j in range(p + 1, 8):
+                pivots[p][j] = pivots[p][j] * inverse
+            for i in range(8):
+                if i != p:
+                    factor = pivots[i][p]
+                    rows[i] = rows[i] - factor * rows[p]
+                    for j in range(p + 1, 8):
+                        pivots[i][j] = pivots[i][j] - factor * pivots[p][j]
+        new = []
+        for g in range(4):
+            terms = [columns[j][g] * rows[j] for j in range(8)]
+            while len(terms) > 1:
+                terms = [terms[n] + terms[n + 1] for n in range(0, len(terms), 2)]
+            new.append(parts[g] - terms[0])
+        for i in range(8):
+            new[own] = jnp.where(sub == i, rows[i], new[own])
         parts = new
     return jnp.concatenate(parts, axis=0)
 
@@ -42,7 +59,7 @@
     ens, cx_in, cy_in, diff_in, cell_in, value_in, noise_in, var_in,
     x_out, e_out,
     halves, q, x1, x2, own_w, own_e, far_w, far_e, next_w, next_e, corner_s, corner_r, crow_s, crow_r, ccol_s, ccol_r,
-    coef, cx, cy, diff, cell, cell16, value, noise, var, id_v, id_s, vn, sw, msg, got,
+    fix_w, fix_e, coef, cx, cy, diff, cell, cell16, value, noise, var, picks, id_v, id_s, msg, got,
     in_sem, out_sem, p1_send, p1_recv, p2_send, p2_recv,
 ):
     la, lo = lax.axis_size("lat"), lax.axis_size("lon")
@@ -87,14 +104,33 @@
         crow_s[side, 0:1, :] = cxv[row : row + 1, :]
         crow_s[side, 1:2, :] = cyv[row : row + 1, :]
     spot = (lax.shift_right_logical(lane, 1) == iota((R, H), 0)) & (lane < 2 * R)
-    for side, col in ((0, C - 1), (1, 0)):
+    even = (lane & 1) == 0
+    for side, col in ((0, C - 2), (1, 0)):
         for n, source in enumerate((cxv, cyv)):
-            spread = jnp.where(spot, jnp.broadcast_to(source[:, col : col + 1], (R, H)), 0.0)
+            pair = [jnp.broadcast_to(source[:, col + c : col + c + 1], (R, H)) for c in range(2)]
+            spread = jnp.where(spot, jnp.where(even, pair[0], pair[1]), 0.0)
             ccol_s[side, n : n + 1, :] = jnp.sum(spread, axis=0, keepdims=True)
 
-    def pack(f):
+    for f in range(F):
         for copy in ens_copies[f]:
             copy.wait()
+
+    def corner_lanes(f):
+        cells = [
+            halves[0, f, pl.ds(0, M, stride=R), :],
+            pltpu.roll(halves[1, f, pl.ds(0, M, stride=R), :], 2, 1),
+            pltpu.roll(halves[0, f, pl.ds(R - 1, M, stride=R), :], 2, 1),
+            pltpu.roll(halves[1, f, pl.ds(R - 1, M, stride=R), :], 4, 1),
+        ]
+        out = jnp.where(lane == 3, cells[3], 0.0)
+        for n in range(3):
+            out = jnp.where(lane == n, cells[n], out)
+        return out
+
+    fill = jnp.zeros((H - F * M, H), jnp.float32)
+    corner_s[...] = jnp.concatenate([corner_lanes(0), corner_lanes(1), fill], axis=0).T[0:8]
+
+    def pack(f):
         def body(r, carry):
             west, east = carry
             c0 = halves[0, f, pl.ds(r, M, stride=R), :]
@@ -119,25 +155,19 @@
             send(COLS + 2 * f + 1, own_w.at[f], far_e.at[f], at(0, -1)),
         ]
 
-    pack(0)
     pl.semaphore_wait(barrier, len(REACH))
-    field_copies = [send_field(0)]
-    halo_copies = [
+    halo_copies = []
+    for n, target in enumerate(((1, 1), (1, -1), (-1, 1), (-1, -1))):
+        halo_copies.append(send(CORNER + n, corner_s, corner_r.at[n], at(*target)))
+    halo_copies += [
         send(CROWS, crow_s.at[0], crow_r.at[0], at(1, 0)),
         send(CROWS + 1, crow_s.at[1], crow_r.at[1], at(-1, 0)),
         send(CCOLS, ccol_s.at[0], ccol_r.at[0], at(0, 1)),
         send(CCOLS + 1, ccol_s.at[1], ccol_r.at[1], at(0, -1)),
     ]
+    pack(0)
+    field_copies = [send_field(0)]
     pack(1)
-    fill = jnp.zeros((H - F * M, H), jnp.float32)
-    turned_w = jnp.concatenate([own_w[0], own_w[1], fill], axis=0).T
-    turned_e = jnp.concatenate([own_e[0], own_e[1], fill], axis=0).T
-    corner_s[0] = turned_e[2 * R - 8 : 2 * R]
-    corner_s[1] = turned_w[2 * R - 8 : 2 * R]
-    corner_s[2] = turned_e[0:8]
-    corner_s[3] = turned_w[0:8]
-    for n, target in enumerate(((1, 1), (1, -1), (-1, 1), (-1, -1))):
-        halo_copies.append(send(CORNER + n, corner_s.at[n], corner_r.at[n], at(*target)))
     field_copies.append(send_field(1))
 
     for copy in o_copies:
@@ -160,24 +190,23 @@
     totals = jnp.broadcast_to(jnp.sum(mask, axis=1, keepdims=True), (n_rows, H))
     rank = dot(mask, before) + dot(rows_before, totals)
     rank = jnp.where(mine, rank, -1.0).astype(jnp.int32)
-    order = lax.shift_right_logical(iota((n_rows, H), 0), 1) * H + iota((n_rows, H), 1)
-    code = jnp.where(mine, (order * R + l_row) * C + l_col, 0).astype(jnp.float32)
+    code = jnp.where(mine, l_row * C + l_col, 0).astype(jnp.float32)
     slot = iota((SLOTS, H), 0)
-    slot_lane = iota((SLOTS, H), 1)
-    columns = []
+    n_copy.wait()
+    picks[...] = jnp.zeros((BATCHES, M + 8, H), jnp.float32)
+    sub_wide = iota((8, count), 0)
     for b in range(BATCHES):
-        acc = [jnp.zeros((SLOTS, H), jnp.float32) for _ in range(3)]
-        for ch in range(chunks):
-            at_row = BATCHES * ch + b
-            here = jnp.broadcast_to(rank[at_row : at_row + 1, :], (SLOTS, H)) == slot
-            cut = slice(ch * H, (ch + 1) * H)
-            for n, source in enumerate((code[at_row : at_row + 1, :], value[b : b + 1, cut], var[b : b + 1, cut])):
-                acc[n] = jnp.where(here, jnp.broadcast_to(source, (SLOTS, H)), acc[n])
-        sums = [jnp.broadcast_to(jnp.sum(a, axis=1, keepdims=True), (SLOTS, H)) for a in acc]
-        id_v[b * SLOTS : (b + 1) * SLOTS, :] = sums[0].astype(jnp.int32)
-        there = sums[2] > 0.0
-        sw[b] = jnp.where(there, jnp.sqrt(1.0 / jnp.where(there, sums[2], 1.0)), 0.0)
-        columns.append(sums[1])
+        rows_b = [BATCHES * ch + b for ch in range(chunks)]
+        chosen = [jnp.where(jnp.broadcast_to(rank[n : n + 1, :], (SLOTS, H)) == slot, 1.0, 0.0) for n in rows_b]
+        code_b = jnp.concatenate([code[n : n + 1, :] for n in rows_b], axis=1)
+        more = jnp.where(sub_wide == 0, jnp.broadcast_to(value[b : b + 1, :], (8, count)), 0.0)
+        more = jnp.where(sub_wide == 1, jnp.broadcast_to(var[b : b + 1, :], (8, count)), more)
+        more = jnp.where(sub_wide == 2, jnp.broadcast_to(code_b, (8, count)), more)
+        picks[b, :, 0:SLOTS] = lax.dot_general(
+            jnp.concatenate([noise[b], more], axis=0), jnp.concatenate(chosen, axis=1),
+            (((1,), (1,)), ((), ())), precision=HI, preferred_element_type=jnp.float32,
+        )
+        id_v[b] = (picks[b, M : M + 8, :] + 0.5).astype(jnp.int32)
     id_copy = load(id_v, id_s, 11)
 
     def parts_of(x, y):
@@ -203,18 +232,50 @@
         north = jnp.where((row_id == R - 1) & high_edge, 0.0, own_parts[3] + rates[f])
         set_coef(f, 8, [centre_of(own_parts, rates[f]), own_parts[0] + rates[f], own_parts[1] + rates[f], south, north])
 
+    def row_step(src, dst, f, r, src_at, dst_at, far, south=True, north=True):
+        first, last = lane == 0, lane == H - 1
+        if far is None:
+            hw = he = jnp.zeros((M, H), jnp.float32)
+        else:
+            turn = (H - 1 - 2 * r) & (H - 1)
+            hw, he = pltpu.roll(far[0], turn, 1), pltpu.roll(far[1], turn, 1)
+        c0, c1 = src[f, r + src_at, :, 0:H], src[f, r + src_at, :, H:C]
+        w0, w1 = pltpu.roll(c0, 1, 1), pltpu.roll(c1, 1, 1)
+        e0, e1 = pltpu.roll(c0, H - 1, 1), pltpu.roll(c1, H - 1, 1)
+        w0, w1 = jnp.where(first, hw, w0), jnp.where(first, w0, w1)
+        e0, e1 = jnp.where(last, e1, e0), jnp.where(last, he, e1)
+        for h, (c, w, e) in enumerate(((c0, w0, e0), (c1, w1, e1))):
+            cut = slice(h * H, (h + 1) * H)
+            rate = [coef[f, n, h, pl.ds(r + 8, 1), :] for n in range(5)]
+            out = rate[0] * c + rate[1] * w + rate[2] * e
+            if south:
+                out = out + rate[3] * src[f, r + src_at - 1, :, cut]
+            if north:
+                out = out + rate[4] * src[f, r + src_at + 1, :, cut]
+            dst[f, r + dst_at, :, cut] = out
+
+    def step_one(f, r):
+        row_step(q, x1, f, r, 2, 1, (far_w[f], far_e[f]))
+
+    def step_two(f, r):
+        row_step(x1, x2, f, r, 1, 0, (next_w[f], next_e[f]))
+
+    def rows_of(step, begin, end):
+        def body(r, carry):
+            step(r)
+            return carry
+
+        lax.fori_loop(begin, end, body, 0, unroll=2)
+
+    def inner(src, dst, src_at, dst_at):
+        row_step(src, dst, 0, 0, src_at, dst_at, None, south=False)
+        rows_of(lambda r: row_step(src, dst, 0, r, src_at, dst_at, None), 1, R - 1)
+        row_step(src, dst, 0, R - 1, src_at, dst_at, None, north=False)
+
+    inner(q, x1, 2, 1)
+    inner(x1, x2, 1, 0)
     id_copy.wait()
-    n_copy.wait()
-    ids = [[id_s[b * SLOTS + s, 0] for s in range(SLOTS)] for b in range(BATCHES)]
-    slot_m = iota((SLOTS, M), 0)
-    move = jnp.where(iota((M, H), 1) == iota((M, H), 0) + M, 1.0, 0.0)
-    middle = (slot_lane >= M) & (slot_lane < 2 * M)
-    for b in range(BATCHES):
-        rows = jnp.zeros((SLOTS, M), jnp.float32)
-        for s in range(SLOTS):
-            one = noise[b, pl.ds(lax.shift_right_logical(ids[b][s], 13) & (count - 1), 1), :]
-            rows = jnp.where(slot_m == s, jnp.broadcast_to(one, (SLOTS, M)), rows)
-        vn[b] = jnp.where(middle, columns[b] + dot(rows, move), 0.0)
+    ids = [[id_s[b, 2, s] for s in range(SLOTS)] for b in range(BATCHES)]
 
     for copy in halo_copies:
         copy.wait_recv()
@@ -222,100 +283,113 @@
     for f in range(F):
         for side, first in ((0, 0), (1, 8 + R)):
             p = halo_rows[side]
-            values = [centre_of(p, rates[f])] + [part + rates[f] for part in p]
-            set_coef(f, first, values)
+            set_coef(f, first, [centre_of(p, rates[f])] + [part + rates[f] for part in p])
     corners = jnp.concatenate([corner_r[n] for n in range(4)] + [jnp.zeros((H - 32, H), jnp.float32)], axis=0).T
+    lane_row = iota((1, H), 1)
+
+    def packed_rates(f, ref, side):
+        p = parts_of(ref[side, 0:1, :], ref[side, 1:2, :])
+        south = jnp.where((lane_row < 2) & low_edge, 0.0, p[2] + rates[f])
+        north = jnp.where((lane_row >= 2 * R - 2) & high_edge, 0.0, p[3] + rates[f])
+        return centre_of(p, rates[f]), p[0] + rates[f], p[1] + rates[f], south, north
 
     def halo_columns(f):
         for copy in field_copies[f][2:]:
             copy.wait_recv()
-        corner = [
-            jnp.broadcast_to(corners[f * M : (f + 1) * M, n : n + 1], (M, H)) for n in (7, 14, 17, 24)
-        ]
+        corner = [jnp.broadcast_to(corners[f * M : (f + 1) * M, n : n + 1], (M, H)) for n in (3, 10, 17, 24)]
         west = far_w[f]
         west = jnp.where(lane == H - 1, corner[0], jnp.where(lane == 2 * R + 1, corner[2], west))
         east = far_e[f]
         east = jnp.where(lane == H - 2, corner[1], jnp.where(lane == 2 * R, corner[3], east))
         far_w[f] = west
         far_e[f] = east
-        lane_row = iota((1, H), 1)
-        for side in range(2):
-            p = parts_of(ccol_r[side, 0:1, :], ccol_r[side, 1:2, :])
-            south = jnp.where((lane_row < 2) & low_edge, 0.0, p[2] + rates[f])
-            north = jnp.where((lane_row >= 2 * R - 2) & high_edge, 0.0, p[3] + rates[f])
-            rate = (centre_of(p, rates[f]), p[0] + rates[f], p[1] + rates[f], south, north)
-            if side == 0:
-                c, w, e = west, pltpu.roll(west, 1, 1), pltpu.roll(own_w[f], 1, 1)
-            else:
-                c, w, e = east, pltpu.roll(own_e[f], H - 1, 1), pltpu.roll(east, H - 1, 1)
+        sides = (
+            (next_w, west, pltpu.roll(west, 1, 1), pltpu.roll(own_w[f], 1, 1)),
+            (next_e, east, pltpu.roll(own_e[f], H - 1, 1), pltpu.roll(east, H - 1, 1)),
+        )
+        for side, (to, c, w, e) in enumerate(sides):
+            rate = packed_rates(f, ccol_r, side)
             out = rate[0] * c + rate[1] * w + rate[2] * e
             out = out + rate[3] * pltpu.roll(c, 2, 1) + rate[4] * pltpu.roll(c, H - 2, 1)
-            out = jnp.where(lane < 2 * R, out, 0.0)
-            if side == 0:
-                next_w[f] = out
-            else:
-                next_e[f] = out
-
-    def row_step(src, dst, f, r, src_at, dst_at, far_west, far_east):
-        turn = (H - 1 - 2 * r) & (H - 1)
-        hw, he = pltpu.roll(far_west, turn, 1), pltpu.roll(far_east, turn, 1)
-        c0, c1 = src[f, r + src_at, :, 0:H], src[f, r + src_at, :, H:C]
-        w0, w1 = pltpu.roll(c0, 1, 1), pltpu.roll(c1, 1, 1)
-        e0, e1 = pltpu.roll(c0, H - 1, 1), pltpu.roll(c1, H - 1, 1)
+            to[f] = jnp.where(lane < 2 * R, out, 0.0)
+
+    def fix_columns():
+        inside = lane < 2 * R
+        for side, to, far, new, outer, turn in (
+            (1, fix_w, far_w, next_w, even, H - 1),
+            (0, fix_e, far_e, next_e, ~even, 1),
+        ):
+            rate = packed_rates(0, ccol_s, side)
+            beside = rate[1] if side == 1 else rate[2]
+            u = jnp.where(inside & outer, beside * pltpu.roll(far[0], turn, 1), 0.0)
+            near = beside * pltpu.roll(new[0], turn, 1) + rate[0] * u
+            near = near + rate[3] * pltpu.roll(u, 2, 1) + rate[4] * pltpu.roll(u, H - 2, 1)
+            to[...] = jnp.where(inside, jnp.where(outer, near, beside * pltpu.roll(u, H - turn, 1)), 0.0)
+
+    def fix_rows():
+        for copy in field_copies[0][:2]:
+            copy.wait_recv()
         first, last = lane == 0, lane == H - 1
-        w0, w1 = jnp.where(first, hw, w0), jnp.where(first, w0, w1)
-        e0, e1 = jnp.where(last, e1, e0), jnp.where(last, he, e1)
-        for h, (c, w, e) in enumerate(((c0, w0, e0), (c1, w1, e1))):
-            cut = slice(h * H, (h + 1) * H)
-            rate = [coef[f, n, h, pl.ds(r + 8, 1), :] for n in range(5)]
-            out = rate[0] * c + rate[1] * w + rate[2] * e
-            out = out + rate[3] * src[f, r + src_at - 1, :, cut] + rate[4] * src[f, r + src_at + 1, :, cut]
-            dst[f, r + dst_at, :, cut] = out
-
-    def step_one(f, r):
-        row_step(q, x1, f, r, 2, 1, far_w[f], far_e[f])
-
-    def step_two(f, r):
-        row_step(x1, x2, f, r, 1, 0, next_w[f], next_e[f])
-
-    def rows_of(step, f, begin, end):
-        def body(r, carry):
-            step(f, r)
-            return carry
-
-        lax.fori_loop(begin, end, body, 0, unroll=2)
-
-    def forecast(f):
-        halo_columns(f)
-        rows_of(step_one, f, 1, R - 1)
-        rows_of(step_two, f, 2, R - 2)
-        for copy in field_copies[f][:2]:
-            copy.wait_recv()
-        for r in (-1, 0, R - 1, R):
-            step_one(f, r)
-        for r in (0, 1, R - 2, R - 1):
-            step_two(f, r)
+        for halo, q_at, x_at, n, row, inner_row in ((-1, 1, 0, 3, 0, 1), (R, R + 2, R + 1, 4, R - 1, R - 2)):
+            step_one(0, halo)
+            rate = [[coef[0, k, h, row + 8 : row + 9, :] for k in range(5)] for h in range(2)]
+            t = [rate[h][n] * q[0, q_at, :, h * H : (h + 1) * H] for h in range(2)]
+            w = [pltpu.roll(v, 1, 1) for v in t]
+            e = [pltpu.roll(v, H - 1, 1) for v in t]
+            w = [jnp.where(first, 0.0, w[0]), jnp.where(first, w[0], w[1])]
+            e = [jnp.where(last, e[1], e[0]), jnp.where(last, 0.0, e[1])]
+            for h in range(2):
+                cut = slice(h * H, (h + 1) * H)
+                add = rate[h][n] * x1[0, x_at, :, cut] + rate[h][0] * t[h] + rate[h][1] * w[h] + rate[h][2] * e[h]
+                x2[0, row, :, cut] = x2[0, row, :, cut] + add
+                x2[0, inner_row, :, cut] = (
+                    x2[0, inner_row, :, cut] + coef[0, n, h, inner_row + 8 : inner_row + 9, :] * t[h]
+                )
+
+    def unpack_columns():
+        def body(r):
+            west = pltpu.roll(fix_w[...], (H - 2 * r) & (H - 1), 1)
+            east = pltpu.roll(fix_e[...], (H - 2 - 2 * r) & (H - 1), 1)
+            x2[0, r, :, 0:H] = x2[0, r, :, 0:H] + jnp.where(lane < 2, west, 0.0)
+            x2[0, r, :, H:C] = x2[0, r, :, H:C] + jnp.where(lane >= H - 2, east, 0.0)
+
+        rows_of(body, 0, R)
+
+    def give(f):
         copy = pltpu.make_async_copy(x2.at[f], x_out.at[f], out_sem.at[f])
         copy.start()
         return copy
 
-    def observe(b):
+    def forecast(f):
+        halo_columns(f)
+        for copy in field_copies[f][:2]:
+            copy.wait_recv()
+        rows_of(lambda r: step_one(f, r), -1, R + 1)
+        rows_of(lambda r: step_two(f, r), 0, R)
+
+    def observe(b, fixes):
         f = b % F
         seen = jnp.zeros((M, H), jnp.float32)
         for s in range(SLOTS):
             code_s = ids[b][s]
-            row = x2[f, lax.shift_right_logical(code_s, 8) & (R - 1)]
+            at_row = lax.shift_right_logical(code_s, 8) & (R - 1)
             col = code_s & (C - 1)
+            row = x2[f, at_row]
             picked = jnp.where(lane == col, row[:, 0:H], 0.0) + jnp.where(lane + H == col, row[:, H:C], 0.0)
+            if fixes:
+                spot_w = jnp.where(col < 2, 2 * at_row + col, -1)
+                spot_e = jnp.where(col >= C - 2, 2 * at_row + col - (C - 2), -1)
+                picked = picked + jnp.where(lane == spot_w, fix_w[...], 0.0) + jnp.where(lane == spot_e, fix_e[...], 0.0)
             seen = jnp.where(lane == s, jnp.broadcast_to(jnp.sum(picked, axis=1, keepdims=True), (M, H)), seen)
         mean = jnp.sum(seen, axis=0, keepdims=True) * (1.0 / M)
-        stacked = jnp.concatenate([seen - mean, seen, jnp.zeros((H - 2 * M, H), jnp.float32)], axis=0)
+        var_b = picks[b, M + 1 : M + 2, :]
+        there = var_b > 0.0
+        scale = jnp.where(there, jnp.sqrt(1.0 / jnp.where(there, var_b, 1.0)), 0.0)
+        innovation = picks[b, M : M + 1, :] + picks[b, 0:M, :] - seen
+        stacked = jnp.concatenate([scale * (seen - mean), scale * innovation, fill], axis=0)
         return stacked.T[0:SLOTS]
 
-    def tell(b, z):
-        signed = jnp.where(slot_lane < M, z, -z)
-        r = sw[b] * (vn[b] + signed)
-        r = jnp.where(slot_lane < 2 * M, r, 0.0)
+    def tell(b, r):
         packed = r[0:8] + pltpu.roll(r[8:16], 2 * M, 1)
         msg[b] = packed
         got[b, 14] = packed
@@ -331,8 +405,6 @@
         started.extend(copies)
         return copies
 
-    lower = iota((8, H), 0)
-
     def transform(b, copies):
         for copy in copies:
             copy.wait_recv()
@@ -351,26 +423,30 @@
         w = jnp.where(lane < M, pltpu.roll(solved, H - M, 1), 0.0)
         return w - jnp.sum(w, axis=0, keepdims=True) * (1.0 / M)
 
-    outs = [forecast(0)]
-    z0 = observe(0)
-    copies0 = tell(0, z0)
-    outs.append(forecast(1))
-    z1 = observe(1)
+    halo_columns(0)
+    fix_columns()
+    fix_rows()
+    copies0 = tell(0, observe(0, True))
+    forecast(1)
+    outs = [give(1)]
+    r1 = observe(1, False)
+    unpack_columns()
+    outs.append(give(0))
     solved0 = transform(0, copies0)
     w0 = jnp.where(lane < M, pltpu.roll(solved0, H - M, 1), 0.0)
     w0_mean = jnp.sum(w0, axis=1, keepdims=True) * (1.0 / M)
-    both0 = jnp.where(lane < M, w0 - w0_mean, jnp.where(lane < 2 * M, solved0, 0.0))
-    z1 = z1 + dot(z1[:, 0:M], both0)
-    copies1 = tell(1, z1)
+    both0 = jnp.where(lane < M, w0 - w0_mean, jnp.where(lane < 2 * M, -solved0, 0.0))
+    copies1 = tell(1, r1 + dot(r1[:, 0:M], both0))
     c0 = centered_rows(solved0)
+    for copy in outs:
+        copy.wait()
+    for copy in started[: -len(REACH)]:
+        copy.wait_send()
     solved1 = transform(1, copies1)
     c1 = centered_rows(solved1)
     e_out[...] = c0 + c1 + dot(c0[:, 0:M], c1)
-
-    for copy in started:
+    for copy in copies1:
         copy.wait_send()
-    for copy in outs:
-        copy.wait()
 
 
 def analysis_kernel(e_ref, x_in, out, x, y, in_sem, out_sem):
@@ -411,7 +487,7 @@
     forecast, combined = pl.pallas_call(
         forecast_kernel,
         out_shape=(jax.ShapeDtypeStruct((F, R, M, C), f32), jax.ShapeDtypeStruct((M, H), f32)),
-        in_specs=[any_space] * 8,
+        in_specs=[pl.BlockSpec(memory_space=pltpu.HBM)] * 8,
         out_specs=(any_space, pl.BlockSpec(memory_space=pltpu.VMEM)),
         scratch_shapes=[
             vmem((2, F, M * R, H), f32),
@@ -424,12 +500,14 @@
             vmem((F, M, H), f32),
             vmem((F, M, H), f32),
             vmem((F, M, H), f32),
-            vmem((4, 8, H), f32),
+            vmem((8, H), f32),
             vmem((4, 8, H), f32),
             vmem((2, 8, C), f32),
             vmem((2, 8, C), f32),
             vmem((2, 8, H), f32),
             vmem((2, 8, H), f32),
+            vmem((M, H), f32),
+            vmem((M, H), f32),
             vmem((F, 5, 2, R + 16, H), f32),
             vmem((R, C), f32),
             vmem((R, C), f32),
@@ -437,12 +515,11 @@
             vmem((BATCHES, count), jnp.int32),
             vmem((BATCHES * count // H, H), jnp.int32),
             vmem((BATCHES, count), f32),
-            vmem((BATCHES, count, M), f32),
+            vmem((BATCHES, M, count), f32),
             vmem((BATCHES, count), f32),
-            vmem((BATCHES * SLOTS, H), jnp.int32),
-            pltpu.SMEM((BATCHES * SLOTS, H), jnp.int32),
-            vmem((BATCHES, SLOTS, H), f32),
-            vmem((BATCHES, SLOTS, H), f32),
+            vmem((BATCHES, M + 8, H), f32),
+            vmem((BATCHES, 8, H), jnp.int32),
+            pltpu.SMEM((BATCHES, 8, H), jnp.int32),
             vmem((BATCHES, 8, H), f32),
             vmem((BATCHES, 16, 8, H), f32),
             dma((12,)),
@@ -456,7 +533,7 @@
             collective_id=0, has_side_effects=True, vmem_limit_bytes=40 * 1024 * 1024
         ),
         name="forecast_and_transform",
-    )(ensemble.reshape(F, M * R, C), courant_x, courant_y, diffusion, obs_cell, obs_value, obs_noise, obs_var)
+    )(ensemble.reshape(F, M * R, C), courant_x, courant_y, diffusion, obs_cell, obs_value, obs_noise.swapaxes(1, 2), obs_var)
     return pl.pallas_call(
         analysis_kernel,
         out_shape=jax.ShapeDtypeStruct((F, M, R, C), f32),

time: 56.4 us -> 48.3 us (0.86)
  Pallas kernels: 48.9 us -> 41.1 us
    pallas_call x1, Pallas kernels: 45.5 us -> 37.7 us  [local(): pl.pallas_call(forecast_kernel, out_shape=(jax.ShapeDtypeStruct((F, R, M,...]
    unnamed x15 -> x16, local copies, waits for them, and re-layouts: 7.12 us -> 6.8 us
where the time goes in v2:
time: 48.3 us; the launch traced here: 47.9 us
  Pallas kernels  41.1 us (85%)
  local copies, waits for them, and re-layouts  6.8 us (14%)
    pallas_call x1, Pallas kernels, local(): pl.pallas_call(forecast_kernel, out_shape=(jax.ShapeDtypeStruct((F, R, M,...  37.7 us
    unnamed x16, local copies, waits for them, and re-layouts  6.8 us
    pallas_call x1, Pallas kernels, local(): pl.pallas_call(analysis_kernel, out_shape=jax.ShapeDtypeStruct((F, M, R,...  3.38 us

profile of v2, /device:TPU:1, one launch (start us, length us, event | category | flops | bytes accessed | tf_op | source)
XLA Modules:
  0.0 47.9 jit_solution(9412414793114540549)
XLA Ops:
  0.0 0.0 copy-start
  0.0 1.6 %copy-done = f32[2,32,32,256]{3,2,1,0:T(8,128)S(1)} copy-done((f32[2,32,32,256]{3,2,1,0:T(8,128)S(1)}, f32[2,32,32,256]{3,2,1,0:T(8,128)}, u32[]{:S(2)}) %copy-start) | copy-done | bytes 2097176
  1.6 0.0 copy-start.1
  1.6 0.9 %copy-done.1 = f32[2,1024,32]{1,2,0:T(8,128)S(1)} copy-done((f32[2,1024,32]{1,2,0:T(8,128)S(1)}, f32[2,1024,32]{1,2,0:T(8,128)}, u32[]{:S(2)}) %copy-start.1) | copy-done | bytes 262168
  2.5 0.0 copy-start.2
  2.5 0.8 %copy-done.2 = f32[32,256]{1,0:T(8,128)S(1)} copy-done((f32[32,256]{1,0:T(8,128)S(1)}, f32[32,256]{1,0:T(8,128)}, u32[]{:S(2)}) %copy-start.2) | copy-done | bytes 32792
  3.3 0.0 copy-start.3
  3.3 0.8 %copy-done.3 = f32[32,256]{1,0:T(8,128)S(1)} copy-done((f32[32,256]{1,0:T(8,128)S(1)}, f32[32,256]{1,0:T(8,128)}, u32[]{:S(2)}) %copy-start.3) | copy-done | bytes 32792
  4.1 0.0 copy-start.4
  4.1 0.7 %copy-done.4 = s32[2,1024]{1,0:T(2,128)S(1)} copy-done((s32[2,1024]{1,0:T(2,128)S(1)}, s32[2,1024]{1,0:T(2,128)}, u32[]{:S(2)}) %copy-start.4) | copy-done | bytes 8216
  4.8 0.0 copy-start.5
  4.8 0.7 %copy-done.5 = f32[2,1024]{1,0:T(2,128)S(1)} copy-done((f32[2,1024]{1,0:T(2,128)S(1)}, f32[2,1024]{1,0:T(2,128)}, u32[]{:S(2)}) %copy-start.5) | copy-done | bytes 8216
  5.5 0.0 copy-start.6
  5.5 0.7 %copy-done.6 = f32[2,1024]{1,0:T(2,128)S(1)} copy-done((f32[2,1024]{1,0:T(2,128)S(1)}, f32[2,1024]{1,0:T(2,128)}, u32[]{:S(2)}) %copy-start.6) | copy-done | bytes 8216
  6.2 0.0 copy-start.7
  6.2 0.7 %copy-done.7 = f32[2]{0:T(128)S(1)} copy-done((f32[2]{0:T(128)S(1)}, f32[2]{0:T(128)}, u32[]{:S(2)}) %copy-start.7) | copy-done | bytes 32
  6.8 37.7 %forecast_and_transform.1 = (f32[2,32,32,256]{3,2,1,0:T(8,128)S(1)}, f32[32,128]{1,0:T(8,128)S(1)}) custom-call(f32[2,1024,256]{2,1,0:T(8,128)S(1)} %bitcast.2, f32[32,256]{1,0:T(8,128)S(1)} %copy-done.2, f32[32,256]{1,0:T(8,128)S(1)} %copy-done.3, f32[2]{0:T(128)S(1)} %copy-done.7, s32[2,1024]{1,0:T(2,128)S(1)} %copy-done.4, f32[2,1024]{1,0:T(2,128)S(1)} %copy-done.5, ...), custom_call_target="tpu_custom_call" | custom-call | tf_op jit(solution)/shard_map/forecast_and_transform/pallas_call | solution.py:487
  44.6 3.4 %analysis.1 = f32[2,32,32,256]{3,2,1,0:T(8,128)} custom-call(f32[32,128]{1,0:T(8,128)S(1)} %get-tuple-element.7.e_ref, f32[2,32,32,256]{3,2,1,0:T(8,128)S(1)} %get-tuple-element.8.x_in), custom_call_target="tpu_custom_call" | custom-call | tf_op jit(solution)/shard_map/analysis/pallas_call | solution.py:537
Async XLA Ops:
  0.0 1.6 %copy-start = (f32[2,32,32,256]{3,2,1,0:T(8,128)S(1)}, f32[2,32,32,256]{3,2,1,0:T(8,128)}, u32[]{:S(2)}) copy-start(f32[2,32,32,256]{3,2,1,0:T(8,128)} %param.9) | copy-start | bytes 6291460
  1.6 0.9 %copy-start.1 = (f32[2,1024,32]{1,2,0:T(8,128)S(1)}, f32[2,1024,32]{1,2,0:T(8,128)}, u32[]{:S(2)}) copy-start(f32[2,1024,32]{1,2,0:T(8,128)} %param.15) | copy-start | bytes 786436
  2.5 0.8 %copy-start.2 = (f32[32,256]{1,0:T(8,128)S(1)}, f32[32,256]{1,0:T(8,128)}, u32[]{:S(2)}) copy-start(f32[32,256]{1,0:T(8,128)} %cx_in.1) | copy-start | bytes 98308
  3.3 0.8 %copy-start.3 = (f32[32,256]{1,0:T(8,128)S(1)}, f32[32,256]{1,0:T(8,128)}, u32[]{:S(2)}) copy-start(f32[32,256]{1,0:T(8,128)} %cy_in.1) | copy-start | bytes 98308
  4.1 0.7 %copy-start.4 = (s32[2,1024]{1,0:T(2,128)S(1)}, s32[2,1024]{1,0:T(2,128)}, u32[]{:S(2)}) copy-start(s32[2,1024]{1,0:T(2,128)} %cell_in.1) | copy-start | bytes 24580
  4.8 0.7 %copy-start.5 = (f32[2,1024]{1,0:T(2,128)S(1)}, f32[2,1024]{1,0:T(2,128)}, u32[]{:S(2)}) copy-start(f32[2,1024]{1,0:T(2,128)} %value_in.1) | copy-start | bytes 24580
  5.5 0.7 %copy-start.6 = (f32[2,1024]{1,0:T(2,128)S(1)}, f32[2,1024]{1,0:T(2,128)}, u32[]{:S(2)}) copy-start(f32[2,1024]{1,0:T(2,128)} %var_in.1) | copy-start | bytes 24580
  6.2 0.7 %copy-start.7 = (f32[2]{0:T(128)S(1)}, f32[2]{0:T(128)}, u32[]{:S(2)}) copy-start(f32[2]{0:T(128)} %diff_in.1) | copy-start | bytes 28

commit v3 on v2

--- a/solution.py
+++ b/solution.py
@@ -11,7 +11,9 @@
 H = 128
 SLOTS = 16
 BATCHES = 2
-REACH = tuple((di, dj) for di in (-1, 0, 1) for dj in range(-2, 3) if (di, dj) != (0, 0))
+GROUP = 16
+REACH = tuple(sorted(((di, dj) for di in (-1, 0, 1) for dj in range(-2, 3) if (di, dj) != (0, 0)), key=lambda d: -abs(d[0]) * 3 - abs(d[1])))
+ADJACENT = tuple(d for d in REACH if abs(d[1]) < 2)
 ROWS, COLS, CORNER, CROWS, CCOLS = 0, 4, 8, 12, 14
 CHANNELS = 16
 
@@ -69,7 +71,7 @@
         return (lax.rem(me_i + (di + la), la), lax.rem(me_j + (dj + lo), lo))
 
     barrier = pltpu.get_barrier_semaphore()
-    for di, dj in REACH:
+    for di, dj in ADJACENT:
         pl.semaphore_signal(barrier, inc=1, device_id=at(di, dj), device_id_type=MESH)
 
     def load(src, dst, sem):
@@ -155,7 +157,9 @@
             send(COLS + 2 * f + 1, own_w.at[f], far_e.at[f], at(0, -1)),
         ]
 
-    pl.semaphore_wait(barrier, len(REACH))
+    pack(0)
+    pack(1)
+    pl.semaphore_wait(barrier, len(ADJACENT))
     halo_copies = []
     for n, target in enumerate(((1, 1), (1, -1), (-1, 1), (-1, -1))):
         halo_copies.append(send(CORNER + n, corner_s, corner_r.at[n], at(*target)))
@@ -165,9 +169,7 @@
         send(CCOLS, ccol_s.at[0], ccol_r.at[0], at(0, 1)),
         send(CCOLS + 1, ccol_s.at[1], ccol_r.at[1], at(0, -1)),
     ]
-    pack(0)
     field_copies = [send_field(0)]
-    pack(1)
     field_copies.append(send_field(1))
 
     for copy in o_copies:
@@ -409,9 +411,11 @@
         for copy in copies:
             copy.wait_recv()
         stack = got[b].reshape(16 * 8, H)
-        place = iota((16 * 8, H), 0)
-        keep = jnp.where(low_edge & (place < 5 * 8), 0.0, 1.0)
-        keep = jnp.where(high_edge & (place >= 9 * 8) & (place < 14 * 8), 0.0, keep)
+        place = lax.shift_right_logical(iota((16 * 8, H), 0), 3)
+        keep = jnp.ones((16 * 8, H), jnp.float32)
+        for n, (di, dj) in enumerate(REACH):
+            if di != 0:
+                keep = jnp.where((low_edge if di < 0 else high_edge) & (place == n), 0.0, keep)
         stack = stack * keep
         turned = stack.T
         gram = dot(jnp.concatenate([turned[0:M], turned[2 * M : 3 * M]], axis=0), stack)
@@ -430,14 +434,14 @@
     forecast(1)
     outs = [give(1)]
     r1 = observe(1, False)
-    unpack_columns()
-    outs.append(give(0))
     solved0 = transform(0, copies0)
     w0 = jnp.where(lane < M, pltpu.roll(solved0, H - M, 1), 0.0)
     w0_mean = jnp.sum(w0, axis=1, keepdims=True) * (1.0 / M)
     both0 = jnp.where(lane < M, w0 - w0_mean, jnp.where(lane < 2 * M, -solved0, 0.0))
     copies1 = tell(1, r1 + dot(r1[:, 0:M], both0))
     c0 = centered_rows(solved0)
+    unpack_columns()
+    outs.append(give(0))
     for copy in outs:
         copy.wait()
     for copy in started[: -len(REACH)]:
@@ -450,10 +454,10 @@
 
 
 def analysis_kernel(e_ref, x_in, out, x, y, in_sem, out_sem):
-    groups = [(f, r) for f in range(F) for r in range(0, R, 8)]
+    groups = [(f, r) for f in range(F) for r in range(0, R, GROUP)]
     loads = []
     for n, (f, r) in enumerate(groups):
-        copy = pltpu.make_async_copy(x_in.at[f, pl.ds(r, 8)], x.at[f, pl.ds(r, 8)], in_sem.at[n])
+        copy = pltpu.make_async_copy(x_in.at[f, pl.ds(r, GROUP)], x.at[f, pl.ds(r, GROUP)], in_sem.at[n])
         copy.start()
         loads.append(copy)
     e = jnp.concatenate([e_ref[...], jnp.zeros((H - M, H), jnp.float32)], axis=0).T[0:M, 0:M]
@@ -463,14 +467,14 @@
     stores = []
     for n, (f, r) in enumerate(groups):
         loads[n].wait()
-        for row in range(r, r + 8):
+        for row in range(r, r + GROUP):
             v = x[f, row]
             hi = v.astype(jnp.bfloat16)
             low = (v - hi.astype(jnp.float32)).astype(jnp.bfloat16)
             right = jnp.concatenate([hi, low, hi], axis=0)
             add = lax.dot_general(left, right, (((1,), (0,)), ((), ())), preferred_element_type=jnp.float32)
             y[f, row] = v + add
-        for row in range(r, r + 8):
+        for row in range(r, r + GROUP):
             copy = pltpu.make_async_copy(y.at[f, row], out.at[f, :, row, :], out_sem.at[f, row])
             copy.start()
             stores.append(copy)
@@ -530,7 +534,7 @@
             dma((BATCHES, len(REACH))),
         ],
         compiler_params=pltpu.CompilerParams(
-            collective_id=0, has_side_effects=True, vmem_limit_bytes=40 * 1024 * 1024
+            collective_id=0, has_side_effects=True, vmem_limit_bytes=60 * 1024 * 1024
         ),
         name="forecast_and_transform",
     )(ensemble.reshape(F, M * R, C), courant_x, courant_y, diffusion, obs_cell, obs_value, obs_noise.swapaxes(1, 2), obs_var)
@@ -542,10 +546,10 @@
         scratch_shapes=[
             vmem((F, R, M, C), f32),
             vmem((F, R, M, C), f32),
-            dma((F * R // 8,)),
+            dma((F * R // GROUP,)),
             dma((F, R)),
         ],
-        compiler_params=pltpu.CompilerParams(vmem_limit_bytes=40 * 1024 * 1024),
+        compiler_params=pltpu.CompilerParams(vmem_limit_bytes=60 * 1024 * 1024),
         name="analysis",
     )(combined, forecast)
 

time: 48.3 us -> 39.9 us (0.83)
  local copies, waits for them, and re-layouts: 6.8 us -> 0 us
  Pallas kernels: 41.1 us -> 39.7 us
    unnamed x16 -> x0, local copies, waits for them, and re-layouts: 6.8 us -> none
    pallas_call x1, Pallas kernels: 37.7 us -> 35.3 us  [local(): pl.pallas_call(forecast_kernel, out_shape=(jax.ShapeDtypeStruct((F, R, M,...]
    pallas_call x1, Pallas kernels: 3.38 us -> 4.37 us  [local(): pl.pallas_call(analysis_kernel, out_shape=jax.ShapeDtypeStruct((F, M, R,...]
where the time goes in v3:
time: 39.9 us; the launch traced here: 39.7 us
  Pallas kernels  39.7 us (99%)
    pallas_call x1, Pallas kernels, local(): pl.pallas_call(forecast_kernel, out_shape=(jax.ShapeDtypeStruct((F, R, M,...  35.3 us
    pallas_call x1, Pallas kernels, local(): pl.pallas_call(analysis_kernel, out_shape=jax.ShapeDtypeStruct((F, M, R,...  4.37 us

profile of v3, /device:TPU:1, one launch (start us, length us, event | category | flops | bytes accessed | tf_op | source)
XLA Modules:
  0.0 39.7 jit_solution(3485315521028275801)
XLA Ops:
  0.0 35.3 %forecast_and_transform.1 = (f32[2,32,32,256]{3,2,1,0:T(8,128)}, f32[32,128]{1,0:T(8,128)}) custom-call(f32[2,1024,256]{2,1,0:T(8,128)} %bitcast.2, f32[32,256]{1,0:T(8,128)} %cx_in.1, f32[32,256]{1,0:T(8,128)} %cy_in.1, f32[2]{0:T(128)} %diff_in.1, s32[2,1024]{1,0:T(2,128)} %cell_in.1, f32[2,1024]{1,0:T(2,128)} %value_in.1, f32[2,32,1024]{2,1,0:T(8,128)} %bitcast.3, ...), custom_call_target="tpu_custom_call" | custom-call | tf_op jit(solution)/shard_map/forecast_and_transform/pallas_call | solution.py:491
  35.3 4.4 %analysis.1 = f32[2,32,32,256]{3,2,1,0:T(8,128)} custom-call(f32[32,128]{1,0:T(8,128)} %get-tuple-element.7.e_ref, f32[2,32,32,256]{3,2,1,0:T(8,128)} %get-tuple-element.8.x_in), custom_call_target="tpu_custom_call" | custom-call | tf_op jit(solution)/shard_map/analysis/pallas_call | solution.py:541

commit v4 on v3

--- a/solution.py
+++ b/solution.py
@@ -59,10 +59,10 @@
 
 def forecast_kernel(
     ens, cx_in, cy_in, diff_in, cell_in, value_in, noise_in, var_in,
-    x_out, e_out,
-    halves, q, x1, x2, own_w, own_e, far_w, far_e, next_w, next_e, corner_s, corner_r, crow_s, crow_r, ccol_s, ccol_r,
+    x2, e_out,
+    halves, q, x1, own_w, own_e, far_w, far_e, next_w, next_e, corner_s, corner_r, crow_s, crow_r, ccol_s, ccol_r,
     fix_w, fix_e, coef, cx, cy, diff, cell, cell16, value, noise, var, picks, id_v, id_s, msg, got,
-    in_sem, out_sem, p1_send, p1_recv, p2_send, p2_recv,
+    in_sem, p1_send, p1_recv, p2_send, p2_recv,
 ):
     la, lo = lax.axis_size("lat"), lax.axis_size("lon")
     me_i, me_j = lax.axis_index("lat"), lax.axis_index("lon")
@@ -357,11 +357,6 @@
 
         rows_of(body, 0, R)
 
-    def give(f):
-        copy = pltpu.make_async_copy(x2.at[f], x_out.at[f], out_sem.at[f])
-        copy.start()
-        return copy
-
     def forecast(f):
         halo_columns(f)
         for copy in field_copies[f][:2]:
@@ -432,7 +427,6 @@
     fix_rows()
     copies0 = tell(0, observe(0, True))
     forecast(1)
-    outs = [give(1)]
     r1 = observe(1, False)
     solved0 = transform(0, copies0)
     w0 = jnp.where(lane < M, pltpu.roll(solved0, H - M, 1), 0.0)
@@ -441,9 +435,6 @@
     copies1 = tell(1, r1 + dot(r1[:, 0:M], both0))
     c0 = centered_rows(solved0)
     unpack_columns()
-    outs.append(give(0))
-    for copy in outs:
-        copy.wait()
     for copy in started[: -len(REACH)]:
         copy.wait_send()
     solved1 = transform(1, copies1)
@@ -453,20 +444,14 @@
         copy.wait_send()
 
 
-def analysis_kernel(e_ref, x_in, out, x, y, in_sem, out_sem):
+def analysis_kernel(e_ref, x, out, y, out_sem):
     groups = [(f, r) for f in range(F) for r in range(0, R, GROUP)]
-    loads = []
-    for n, (f, r) in enumerate(groups):
-        copy = pltpu.make_async_copy(x_in.at[f, pl.ds(r, GROUP)], x.at[f, pl.ds(r, GROUP)], in_sem.at[n])
-        copy.start()
-        loads.append(copy)
     e = jnp.concatenate([e_ref[...], jnp.zeros((H - M, H), jnp.float32)], axis=0).T[0:M, 0:M]
     e_hi = e.astype(jnp.bfloat16)
     e_lo = (e - e_hi.astype(jnp.float32)).astype(jnp.bfloat16)
     left = jnp.concatenate([e_hi, e_hi, e_lo], axis=1)
     stores = []
-    for n, (f, r) in enumerate(groups):
-        loads[n].wait()
+    for f, r in groups:
         for row in range(r, r + GROUP):
             v = x[f, row]
             hi = v.astype(jnp.bfloat16)
@@ -488,16 +473,19 @@
     count = obs_cell.shape[1]
     vmem = pltpu.VMEM
     dma = pltpu.SemaphoreType.DMA
+    noise_turned = obs_noise.swapaxes(1, 2)
+    operands = (
+        ensemble.reshape(F, M * R, C), courant_x, courant_y, diffusion, obs_cell, obs_value, noise_turned, obs_var
+    )
     forecast, combined = pl.pallas_call(
         forecast_kernel,
-        out_shape=(jax.ShapeDtypeStruct((F, R, M, C), f32), jax.ShapeDtypeStruct((M, H), f32)),
+        out_shape=(vmem((F, R, M, C), f32), vmem((M, H), f32)),
         in_specs=[pl.BlockSpec(memory_space=pltpu.HBM)] * 8,
-        out_specs=(any_space, pl.BlockSpec(memory_space=pltpu.VMEM)),
+        out_specs=(pl.BlockSpec(memory_space=pltpu.VMEM), pl.BlockSpec(memory_space=pltpu.VMEM)),
         scratch_shapes=[
             vmem((2, F, M * R, H), f32),
             vmem((F, R + 4, M, C), f32),
             vmem((F, R + 2, M, C), f32),
-            vmem((F, R, M, C), f32),
             vmem((F, M, H), f32),
             vmem((F, M, H), f32),
             vmem((F, M, H), f32),
@@ -527,31 +515,28 @@
             vmem((BATCHES, 8, H), f32),
             vmem((BATCHES, 16, 8, H), f32),
             dma((12,)),
-            dma((F,)),
             dma((CHANNELS,)),
             dma((CHANNELS,)),
             dma((BATCHES, len(REACH))),
             dma((BATCHES, len(REACH))),
         ],
         compiler_params=pltpu.CompilerParams(
-            collective_id=0, has_side_effects=True, vmem_limit_bytes=60 * 1024 * 1024
+            collective_id=0, has_side_effects=True, vmem_limit_bytes=48 * 1024 * 1024
         ),
         name="forecast_and_transform",
-    )(ensemble.reshape(F, M * R, C), courant_x, courant_y, diffusion, obs_cell, obs_value, obs_noise.swapaxes(1, 2), obs_var)
+    )(*(pltpu.with_memory_space_constraint(a, pltpu.HBM) for a in operands))
     return pl.pallas_call(
         analysis_kernel,
         out_shape=jax.ShapeDtypeStruct((F, M, R, C), f32),
-        in_specs=[pl.BlockSpec(memory_space=pltpu.VMEM), any_space],
+        in_specs=[pl.BlockSpec(memory_space=pltpu.VMEM)] * 2,
         out_specs=any_space,
         scratch_shapes=[
             vmem((F, R, M, C), f32),
-            vmem((F, R, M, C), f32),
-            dma((F * R // GROUP,)),
             dma((F, R)),
         ],
-        compiler_params=pltpu.CompilerParams(vmem_limit_bytes=60 * 1024 * 1024),
+        compiler_params=pltpu.CompilerParams(vmem_limit_bytes=48 * 1024 * 1024),
         name="analysis",
-    )(combined, forecast)
+    )(*(pltpu.with_memory_space_constraint(a, pltpu.VMEM) for a in (combined, forecast)))
 
 
 def solution(mesh):

time: 39.9 us -> 37.7 us (0.945)
  Pallas kernels: 39.7 us -> 37.6 us
    pallas_call x1, Pallas kernels: 4.37 us -> 2.7 us  [local(): pl.pallas_call(analysis_kernel, out_shape=jax.ShapeDtypeStruct((F, M, R,...]
    pallas_call x1, Pallas kernels: 35.3 us -> 34.9 us  [local(): pl.pallas_call(forecast_kernel, out_shape=(vmem((F, R, M, C), f32), vmem(...]
where the time goes in v4:
time: 37.7 us; the launch traced here: 37.6 us
  Pallas kernels  37.6 us (100%)
    pallas_call x1, Pallas kernels, local(): pl.pallas_call(forecast_kernel, out_shape=(vmem((F, R, M, C), f32), vmem(...  34.9 us
    pallas_call x1, Pallas kernels, local(): pl.pallas_call(analysis_kernel, out_shape=jax.ShapeDtypeStruct((F, M, R,...  2.7 us

profile of v4, /device:TPU:1, one launch (start us, length us, event | category | flops | bytes accessed | tf_op | source)
XLA Modules:
  0.0 37.6 jit_solution(2843094748393131249)
XLA Ops:
  0.0 34.9 %forecast_and_transform.1 = (f32[2,32,32,256]{3,2,1,0:T(8,128)S(1)}, f32[32,128]{1,0:T(8,128)S(1)}) custom-call(f32[2,1024,256]{2,1,0:T(8,128)} %bitcast.2, f32[32,256]{1,0:T(8,128)} %cx_in.1, f32[32,256]{1,0:T(8,128)} %cy_in.1, f32[2]{0:T(128)} %diff_in.1, s32[2,1024]{1,0:T(2,128)} %cell_in.1, f32[2,1024]{1,0:T(2,128)} %value_in.1, f32[2,32,1024]{2,1,0:T(8,128)} %bitcast.3, ...), custom_call_target="tpu_custom_call" | custom-call | tf_op jit(solution)/shard_map/forecast_and_transform/pallas_call | solution.py:480
  34.9 2.7 %analysis.1 = f32[2,32,32,256]{3,2,1,0:T(8,128)} custom-call(f32[32,128]{1,0:T(8,128)S(1)} %get-tuple-element.7.e_ref, f32[2,32,32,256]{3,2,1,0:T(8,128)S(1)} %get-tuple-element.8.x), custom_call_target="tpu_custom_call" | custom-call | tf_op jit(solution)/shard_map/analysis/pallas_call | solution.py:528

commit v5 on v4

--- a/solution.py
+++ b/solution.py
@@ -14,8 +14,8 @@
 GROUP = 16
 REACH = tuple(sorted(((di, dj) for di in (-1, 0, 1) for dj in range(-2, 3) if (di, dj) != (0, 0)), key=lambda d: -abs(d[0]) * 3 - abs(d[1])))
 ADJACENT = tuple(d for d in REACH if abs(d[1]) < 2)
-ROWS, COLS, CORNER, CROWS, CCOLS = 0, 4, 8, 12, 14
-CHANNELS = 16
+ROWS, COLS, CORNER, CROWS, CCOLS = 0, 2, 4, 5, 6
+CHANNELS = 7
 
 
 def iota(shape, axis):
@@ -60,8 +60,8 @@
 def forecast_kernel(
     ens, cx_in, cy_in, diff_in, cell_in, value_in, noise_in, var_in,
     x2, e_out,
-    halves, q, x1, own_w, own_e, far_w, far_e, next_w, next_e, corner_s, corner_r, crow_s, crow_r, ccol_s, ccol_r,
-    fix_w, fix_e, coef, cx, cy, diff, cell, cell16, value, noise, var, picks, id_v, id_s, msg, got,
+    halves, q, x1, own_w, own_e, far, next_w, next_e, corner_s, corner_r, crow_s, crow_r, ccol_s, ccol_r,
+    fix_w, fix_e, coef, courant, diff, cell, cell16, value, noise, picks, id_v, id_s, msg, got,
     in_sem, p1_send, p1_recv, p2_send, p2_recv,
 ):
     la, lo = lax.axis_size("lat"), lax.axis_size("lon")
@@ -79,29 +79,38 @@
         copy.start()
         return copy
 
-    ens_copies = [
-        [load(ens.at[f, :, pl.ds(h * H, H)], halves.at[h, f], 2 * f + h) for h in range(2)] for f in range(F)
-    ]
-    c_copies = [load(cx_in, cx, 4), load(cy_in, cy, 5), load(diff_in, diff, 6)]
-    o_copies = [load(cell_in, cell, 7), load(value_in, value, 8), load(var_in, var, 9)]
-    n_copy = load(noise_in, noise, 10)
+    def loaded(dst, sem):
+        pltpu.make_async_copy(dst, dst, in_sem.at[sem]).wait()
+
+    for f in range(F):
+        for h in range(2):
+            load(ens.at[f, :, pl.ds(h * H, H)], halves.at[h, f], 0)
+    load(cx_in, courant.at[0], 1)
+    load(cy_in, courant.at[1], 1)
+    diff_copy = load(diff_in, diff, 2)
+    cell_copy = load(cell_in, cell, 3)
+    load(value_in, value.at[0], 4)
+    load(var_in, value.at[1], 4)
+    noise_copy = load(noise_in, noise, 5)
 
     lane = iota((M, H), 1)
     lane8 = iota((8, H), 1)
-    started = []
-
     def send(channel, src, dst, target):
         copy = pltpu.make_async_remote_copy(
             src_ref=src, dst_ref=dst, send_sem=p1_send.at[channel], recv_sem=p1_recv.at[channel],
             device_id=target, device_id_type=MESH,
         )
         copy.start()
-        started.append(copy)
-        return copy
-
-    for copy in c_copies:
-        copy.wait()
-    cxv, cyv = cx[...], cy[...]
+
+    def sent(src, channel):
+        pltpu.make_async_copy(src, src, p1_send.at[channel]).wait()
+
+    def came(dst, channel):
+        pltpu.make_async_copy(dst, dst, p1_recv.at[channel]).wait()
+
+    loaded(courant, 1)
+    diff_copy.wait()
+    cxv, cyv = courant[0], courant[1]
     for side, row in ((0, R - 1), (1, 0)):
         crow_s[side, 0:1, :] = cxv[row : row + 1, :]
         crow_s[side, 1:2, :] = cyv[row : row + 1, :]
@@ -113,9 +122,7 @@
             spread = jnp.where(spot, jnp.where(even, pair[0], pair[1]), 0.0)
             ccol_s[side, n : n + 1, :] = jnp.sum(spread, axis=0, keepdims=True)
 
-    for f in range(F):
-        for copy in ens_copies[f]:
-            copy.wait()
+    loaded(halves, 0)
 
     def corner_lanes(f):
         cells = [
@@ -150,30 +157,24 @@
         own_e[f] = east
 
     def send_field(f):
-        return [
-            send(ROWS + 2 * f, q.at[f, pl.ds(R, 2)], q.at[f, pl.ds(0, 2)], at(1, 0)),
-            send(ROWS + 2 * f + 1, q.at[f, pl.ds(2, 2)], q.at[f, pl.ds(R + 2, 2)], at(-1, 0)),
-            send(COLS + 2 * f, own_e.at[f], far_w.at[f], at(0, 1)),
-            send(COLS + 2 * f + 1, own_w.at[f], far_e.at[f], at(0, -1)),
-        ]
+        send(COLS + f, own_e.at[f], far.at[f, 0], at(0, 1))
+        send(COLS + f, own_w.at[f], far.at[f, 1], at(0, -1))
+        send(ROWS + f, q.at[f, pl.ds(R, 2)], q.at[f, pl.ds(0, 2)], at(1, 0))
+        send(ROWS + f, q.at[f, pl.ds(2, 2)], q.at[f, pl.ds(R + 2, 2)], at(-1, 0))
 
     pack(0)
     pack(1)
     pl.semaphore_wait(barrier, len(ADJACENT))
-    halo_copies = []
     for n, target in enumerate(((1, 1), (1, -1), (-1, 1), (-1, -1))):
-        halo_copies.append(send(CORNER + n, corner_s, corner_r.at[n], at(*target)))
-    halo_copies += [
-        send(CROWS, crow_s.at[0], crow_r.at[0], at(1, 0)),
-        send(CROWS + 1, crow_s.at[1], crow_r.at[1], at(-1, 0)),
-        send(CCOLS, ccol_s.at[0], ccol_r.at[0], at(0, 1)),
-        send(CCOLS + 1, ccol_s.at[1], ccol_r.at[1], at(0, -1)),
-    ]
-    field_copies = [send_field(0)]
-    field_copies.append(send_field(1))
-
-    for copy in o_copies:
-        copy.wait()
+        send(CORNER, corner_s, corner_r.at[n], at(*target))
+    send(CROWS, crow_s.at[0], crow_r.at[0], at(1, 0))
+    send(CROWS, crow_s.at[1], crow_r.at[1], at(-1, 0))
+    send(CCOLS, ccol_s.at[0], ccol_r.at[0], at(0, 1))
+    send(CCOLS, ccol_s.at[1], ccol_r.at[1], at(0, -1))
+    send_field(0)
+
+    cell_copy.wait()
+    loaded(value, 4)
     count = cell.shape[1]
     chunks = count // H
     wide = lo * C
@@ -194,22 +195,22 @@
     rank = jnp.where(mine, rank, -1.0).astype(jnp.int32)
     code = jnp.where(mine, l_row * C + l_col, 0).astype(jnp.float32)
     slot = iota((SLOTS, H), 0)
-    n_copy.wait()
+    noise_copy.wait()
     picks[...] = jnp.zeros((BATCHES, M + 8, H), jnp.float32)
     sub_wide = iota((8, count), 0)
     for b in range(BATCHES):
         rows_b = [BATCHES * ch + b for ch in range(chunks)]
         chosen = [jnp.where(jnp.broadcast_to(rank[n : n + 1, :], (SLOTS, H)) == slot, 1.0, 0.0) for n in rows_b]
         code_b = jnp.concatenate([code[n : n + 1, :] for n in rows_b], axis=1)
-        more = jnp.where(sub_wide == 0, jnp.broadcast_to(value[b : b + 1, :], (8, count)), 0.0)
-        more = jnp.where(sub_wide == 1, jnp.broadcast_to(var[b : b + 1, :], (8, count)), more)
+        more = jnp.where(sub_wide == 0, jnp.broadcast_to(value[0, b : b + 1, :], (8, count)), 0.0)
+        more = jnp.where(sub_wide == 1, jnp.broadcast_to(value[1, b : b + 1, :], (8, count)), more)
         more = jnp.where(sub_wide == 2, jnp.broadcast_to(code_b, (8, count)), more)
         picks[b, :, 0:SLOTS] = lax.dot_general(
             jnp.concatenate([noise[b], more], axis=0), jnp.concatenate(chosen, axis=1),
             (((1,), (1,)), ((), ())), precision=HI, preferred_element_type=jnp.float32,
         )
         id_v[b] = (picks[b, M : M + 8, :] + 0.5).astype(jnp.int32)
-    id_copy = load(id_v, id_s, 11)
+    id_copy = load(id_v, id_s, 6)
 
     def parts_of(x, y):
         return jnp.maximum(x, 0.0), -jnp.minimum(x, 0.0), jnp.maximum(y, 0.0), -jnp.minimum(y, 0.0)
@@ -257,10 +258,7 @@
             dst[f, r + dst_at, :, cut] = out
 
     def step_one(f, r):
-        row_step(q, x1, f, r, 2, 1, (far_w[f], far_e[f]))
-
-    def step_two(f, r):
-        row_step(x1, x2, f, r, 1, 0, (next_w[f], next_e[f]))
+        row_step(q, x1, f, r, 2, 1, (far[f, 0], far[f, 1]))
 
     def rows_of(step, begin, end):
         def body(r, carry):
@@ -269,23 +267,25 @@
 
         lax.fori_loop(begin, end, body, 0, unroll=2)
 
-    def inner(src, dst, src_at, dst_at):
-        row_step(src, dst, 0, 0, src_at, dst_at, None, south=False)
-        rows_of(lambda r: row_step(src, dst, 0, r, src_at, dst_at, None), 1, R - 1)
-        row_step(src, dst, 0, R - 1, src_at, dst_at, None, north=False)
-
-    inner(q, x1, 2, 1)
-    inner(x1, x2, 1, 0)
+    def inner(f, src, dst, src_at, dst_at):
+        row_step(src, dst, f, 0, src_at, dst_at, None, south=False)
+        rows_of(lambda r: row_step(src, dst, f, r, src_at, dst_at, None), 1, R - 1)
+        row_step(src, dst, f, R - 1, src_at, dst_at, None, north=False)
+
+    inner(0, q, x1, 2, 1)
+    send_field(1)
+    inner(0, x1, x2, 1, 0)
     id_copy.wait()
     ids = [[id_s[b, 2, s] for s in range(SLOTS)] for b in range(BATCHES)]
 
-    for copy in halo_copies:
-        copy.wait_recv()
+    came(crow_r, CROWS)
+    came(ccol_r, CCOLS)
     halo_rows = [parts_of(crow_r[side, 0:1, :], crow_r[side, 1:2, :]) for side in range(2)]
     for f in range(F):
         for side, first in ((0, 0), (1, 8 + R)):
             p = halo_rows[side]
             set_coef(f, first, [centre_of(p, rates[f])] + [part + rates[f] for part in p])
+    came(corner_r, CORNER)
     corners = jnp.concatenate([corner_r[n] for n in range(4)] + [jnp.zeros((H - 32, H), jnp.float32)], axis=0).T
     lane_row = iota((1, H), 1)
 
@@ -296,15 +296,14 @@
         return centre_of(p, rates[f]), p[0] + rates[f], p[1] + rates[f], south, north
 
     def halo_columns(f):
-        for copy in field_copies[f][2:]:
-            copy.wait_recv()
+        came(far.at[f], COLS + f)
         corner = [jnp.broadcast_to(corners[f * M : (f + 1) * M, n : n + 1], (M, H)) for n in (3, 10, 17, 24)]
-        west = far_w[f]
+        west = far[f, 0]
         west = jnp.where(lane == H - 1, corner[0], jnp.where(lane == 2 * R + 1, corner[2], west))
-        east = far_e[f]
+        east = far[f, 1]
         east = jnp.where(lane == H - 2, corner[1], jnp.where(lane == 2 * R, corner[3], east))
-        far_w[f] = west
-        far_e[f] = east
+        far[f, 0] = west
+        far[f, 1] = east
         sides = (
             (next_w, west, pltpu.roll(west, 1, 1), pltpu.roll(own_w[f], 1, 1)),
             (next_e, east, pltpu.roll(own_e[f], H - 1, 1), pltpu.roll(east, H - 1, 1)),
@@ -315,56 +314,48 @@
             out = out + rate[3] * pltpu.roll(c, 2, 1) + rate[4] * pltpu.roll(c, H - 2, 1)
             to[f] = jnp.where(lane < 2 * R, out, 0.0)
 
-    def fix_columns():
+    def fix_columns(f):
         inside = lane < 2 * R
-        for side, to, far, new, outer, turn in (
-            (1, fix_w, far_w, next_w, even, H - 1),
-            (0, fix_e, far_e, next_e, ~even, 1),
+        for side, to, outside, new, outer, turn in (
+            (1, fix_w, far[f, 0], next_w, even, H - 1),
+            (0, fix_e, far[f, 1], next_e, ~even, 1),
         ):
-            rate = packed_rates(0, ccol_s, side)
+            rate = packed_rates(f, ccol_s, side)
             beside = rate[1] if side == 1 else rate[2]
-            u = jnp.where(inside & outer, beside * pltpu.roll(far[0], turn, 1), 0.0)
-            near = beside * pltpu.roll(new[0], turn, 1) + rate[0] * u
+            u = jnp.where(inside & outer, beside * pltpu.roll(outside, turn, 1), 0.0)
+            near = beside * pltpu.roll(new[f], turn, 1) + rate[0] * u
             near = near + rate[3] * pltpu.roll(u, 2, 1) + rate[4] * pltpu.roll(u, H - 2, 1)
-            to[...] = jnp.where(inside, jnp.where(outer, near, beside * pltpu.roll(u, H - turn, 1)), 0.0)
-
-    def fix_rows():
-        for copy in field_copies[0][:2]:
-            copy.wait_recv()
+            to[f] = jnp.where(inside, jnp.where(outer, near, beside * pltpu.roll(u, H - turn, 1)), 0.0)
+
+    def fix_rows(f):
+        came(q.at[f, pl.ds(0, 4)], ROWS + f)
         first, last = lane == 0, lane == H - 1
         for halo, q_at, x_at, n, row, inner_row in ((-1, 1, 0, 3, 0, 1), (R, R + 2, R + 1, 4, R - 1, R - 2)):
-            step_one(0, halo)
-            rate = [[coef[0, k, h, row + 8 : row + 9, :] for k in range(5)] for h in range(2)]
-            t = [rate[h][n] * q[0, q_at, :, h * H : (h + 1) * H] for h in range(2)]
+            step_one(f, halo)
+            rate = [[coef[f, k, h, row + 8 : row + 9, :] for k in range(5)] for h in range(2)]
+            t = [rate[h][n] * q[f, q_at, :, h * H : (h + 1) * H] for h in range(2)]
             w = [pltpu.roll(v, 1, 1) for v in t]
             e = [pltpu.roll(v, H - 1, 1) for v in t]
             w = [jnp.where(first, 0.0, w[0]), jnp.where(first, w[0], w[1])]
             e = [jnp.where(last, e[1], e[0]), jnp.where(last, 0.0, e[1])]
             for h in range(2):
                 cut = slice(h * H, (h + 1) * H)
-                add = rate[h][n] * x1[0, x_at, :, cut] + rate[h][0] * t[h] + rate[h][1] * w[h] + rate[h][2] * e[h]
-                x2[0, row, :, cut] = x2[0, row, :, cut] + add
-                x2[0, inner_row, :, cut] = (
-                    x2[0, inner_row, :, cut] + coef[0, n, h, inner_row + 8 : inner_row + 9, :] * t[h]
+                add = rate[h][n] * x1[f, x_at, :, cut] + rate[h][0] * t[h] + rate[h][1] * w[h] + rate[h][2] * e[h]
+                x2[f, row, :, cut] = x2[f, row, :, cut] + add
+                x2[f, inner_row, :, cut] = (
+                    x2[f, inner_row, :, cut] + coef[f, n, h, inner_row + 8 : inner_row + 9, :] * t[h]
                 )
 
-    def unpack_columns():
+    def unpack_columns(f):
         def body(r):
-            west = pltpu.roll(fix_w[...], (H - 2 * r) & (H - 1), 1)
-            east = pltpu.roll(fix_e[...], (H - 2 - 2 * r) & (H - 1), 1)
-            x2[0, r, :, 0:H] = x2[0, r, :, 0:H] + jnp.where(lane < 2, west, 0.0)
-            x2[0, r, :, H:C] = x2[0, r, :, H:C] + jnp.where(lane >= H - 2, east, 0.0)
+            west = pltpu.roll(fix_w[f], (H - 2 * r) & (H - 1), 1)
+            east = pltpu.roll(fix_e[f], (H - 2 - 2 * r) & (H - 1), 1)
+            x2[f, r, :, 0:H] = x2[f, r, :, 0:H] + jnp.where(lane < 2, west, 0.0)
+            x2[f, r, :, H:C] = x2[f, r, :, H:C] + jnp.where(lane >= H - 2, east, 0.0)
 
         rows_of(body, 0, R)
 
-    def forecast(f):
-        halo_columns(f)
-        for copy in field_copies[f][:2]:
-            copy.wait_recv()
-        rows_of(lambda r: step_one(f, r), -1, R + 1)
-        rows_of(lambda r: step_two(f, r), 0, R)
-
-    def observe(b, fixes):
+    def observe(b):
         f = b % F
         seen = jnp.zeros((M, H), jnp.float32)
         for s in range(SLOTS):
@@ -373,10 +364,9 @@
             col = code_s & (C - 1)
             row = x2[f, at_row]
             picked = jnp.where(lane == col, row[:, 0:H], 0.0) + jnp.where(lane + H == col, row[:, H:C], 0.0)
-            if fixes:
-                spot_w = jnp.where(col < 2, 2 * at_row + col, -1)
-                spot_e = jnp.where(col >= C - 2, 2 * at_row + col - (C - 2), -1)
-                picked = picked + jnp.where(lane == spot_w, fix_w[...], 0.0) + jnp.where(lane == spot_e, fix_e[...], 0.0)
+            spot_w = jnp.where(col < 2, 2 * at_row + col, -1)
+            spot_e = jnp.where(col >= C - 2, 2 * at_row + col - (C - 2), -1)
+            picked = picked + jnp.where(lane == spot_w, fix_w[f], 0.0) + jnp.where(lane == spot_e, fix_e[f], 0.0)
             seen = jnp.where(lane == s, jnp.broadcast_to(jnp.sum(picked, axis=1, keepdims=True), (M, H)), seen)
         mean = jnp.sum(seen, axis=0, keepdims=True) * (1.0 / M)
         var_b = picks[b, M + 1 : M + 2, :]
@@ -391,20 +381,15 @@
         msg[b] = packed
         got[b, 14] = packed
         got[b, 15] = jnp.zeros((8, H), jnp.float32)
-        copies = []
         for n, (di, dj) in enumerate(REACH):
-            copy = pltpu.make_async_remote_copy(
-                src_ref=msg.at[b], dst_ref=got.at[b, n], send_sem=p2_send.at[b, n], recv_sem=p2_recv.at[b, n],
+            pltpu.make_async_remote_copy(
+                src_ref=msg.at[b], dst_ref=got.at[b, n], send_sem=p2_send.at[b], recv_sem=p2_recv.at[b],
                 device_id=at(-di, -dj), device_id_type=MESH,
-            )
-            copy.start()
-            copies.append(copy)
-        started.extend(copies)
-        return copies
-
-    def transform(b, copies):
-        for copy in copies:
-            copy.wait_recv()
+            ).start()
+
+    def transform(b):
+        others = got.at[b, pl.ds(0, len(REACH))]
+        pltpu.make_async_copy(others, others, p2_recv.at[b]).wait()
         stack = got[b].reshape(16 * 8, H)
         place = lax.shift_right_logical(iota((16 * 8, H), 0), 3)
         keep = jnp.ones((16 * 8, H), jnp.float32)
@@ -423,25 +408,35 @@
         return w - jnp.sum(w, axis=0, keepdims=True) * (1.0 / M)
 
     halo_columns(0)
-    fix_columns()
-    fix_rows()
-    copies0 = tell(0, observe(0, True))
-    forecast(1)
-    r1 = observe(1, False)
-    solved0 = transform(0, copies0)
+    fix_columns(0)
+    fix_rows(0)
+    tell(0, observe(0))
+    inner(1, q, x1, 2, 1)
+    inner(1, x1, x2, 1, 0)
+    halo_columns(1)
+    fix_columns(1)
+    fix_rows(1)
+    r1 = observe(1)
+    solved0 = transform(0)
     w0 = jnp.where(lane < M, pltpu.roll(solved0, H - M, 1), 0.0)
     w0_mean = jnp.sum(w0, axis=1, keepdims=True) * (1.0 / M)
     both0 = jnp.where(lane < M, w0 - w0_mean, jnp.where(lane < 2 * M, -solved0, 0.0))
-    copies1 = tell(1, r1 + dot(r1[:, 0:M], both0))
+    tell(1, r1 + dot(r1[:, 0:M], both0))
     c0 = centered_rows(solved0)
-    unpack_columns()
-    for copy in started[: -len(REACH)]:
-        copy.wait_send()
-    solved1 = transform(1, copies1)
+    unpack_columns(0)
+    unpack_columns(1)
+    for f in range(F):
+        sent(q.at[f, pl.ds(2, 4)], ROWS + f)
+        sent(far.at[f], COLS + f)
+    sent(corner_r, CORNER)
+    sent(crow_s, CROWS)
+    sent(ccol_s, CCOLS)
+    solved1 = transform(1)
     c1 = centered_rows(solved1)
     e_out[...] = c0 + c1 + dot(c0[:, 0:M], c1)
-    for copy in copies1:
-        copy.wait_send()
+    for b in range(BATCHES):
+        others = got.at[b, pl.ds(0, len(REACH))]
+        pltpu.make_async_copy(others, others, p2_send.at[b]).wait()
 
 
 def analysis_kernel(e_ref, x, out, y, out_sem):
@@ -450,7 +445,6 @@
     e_hi = e.astype(jnp.bfloat16)
     e_lo = (e - e_hi.astype(jnp.float32)).astype(jnp.bfloat16)
     left = jnp.concatenate([e_hi, e_hi, e_lo], axis=1)
-    stores = []
     for f, r in groups:
         for row in range(r, r + GROUP):
             v = x[f, row]
@@ -460,11 +454,8 @@
             add = lax.dot_general(left, right, (((1,), (0,)), ((), ())), preferred_element_type=jnp.float32)
             y[f, row] = v + add
         for row in range(r, r + GROUP):
-            copy = pltpu.make_async_copy(y.at[f, row], out.at[f, :, row, :], out_sem.at[f, row])
-            copy.start()
-            stores.append(copy)
-    for copy in stores:
-        copy.wait()
+            pltpu.make_async_copy(y.at[f, row], out.at[f, :, row, :], out_sem).start()
+    pltpu.make_async_copy(y, y, out_sem).wait()
 
 
 def local(ensemble, courant_x, courant_y, diffusion, obs_cell, obs_value, obs_noise, obs_var, loc_mask):
@@ -488,8 +479,7 @@
             vmem((F, R + 2, M, C), f32),
             vmem((F, M, H), f32),
             vmem((F, M, H), f32),
-            vmem((F, M, H), f32),
-            vmem((F, M, H), f32),
+            vmem((F, 2, M, H), f32),
             vmem((F, M, H), f32),
             vmem((F, M, H), f32),
             vmem((8, H), f32),
@@ -498,27 +488,25 @@
             vmem((2, 8, C), f32),
             vmem((2, 8, H), f32),
             vmem((2, 8, H), f32),
-            vmem((M, H), f32),
-            vmem((M, H), f32),
+            vmem((F, M, H), f32),
+            vmem((F, M, H), f32),
             vmem((F, 5, 2, R + 16, H), f32),
-            vmem((R, C), f32),
-            vmem((R, C), f32),
+            vmem((2, R, C), f32),
             pltpu.SMEM((F,), f32),
             vmem((BATCHES, count), jnp.int32),
             vmem((BATCHES * count // H, H), jnp.int32),
-            vmem((BATCHES, count), f32),
+            vmem((2, BATCHES, count), f32),
             vmem((BATCHES, M, count), f32),
-            vmem((BATCHES, count), f32),
             vmem((BATCHES, M + 8, H), f32),
             vmem((BATCHES, 8, H), jnp.int32),
             pltpu.SMEM((BATCHES, 8, H), jnp.int32),
             vmem((BATCHES, 8, H), f32),
             vmem((BATCHES, 16, 8, H), f32),
-            dma((12,)),
+            dma((7,)),
             dma((CHANNELS,)),
             dma((CHANNELS,)),
-            dma((BATCHES, len(REACH))),
-            dma((BATCHES, len(REACH))),
+            dma((BATCHES,)),
+            dma((BATCHES,)),
         ],
         compiler_params=pltpu.CompilerParams(
             collective_id=0, has_side_effects=True, vmem_limit_bytes=48 * 1024 * 1024
@@ -532,7 +520,7 @@
         out_specs=any_space,
         scratch_shapes=[
             vmem((F, R, M, C), f32),
-            dma((F, R)),
+            dma,
         ],
         compiler_params=pltpu.CompilerParams(vmem_limit_bytes=48 * 1024 * 1024),
         name="analysis",

time: 37.7 us -> 35.5 us (0.942)
  Pallas kernels: 37.6 us -> 35.4 us
    pallas_call x1, Pallas kernels: 34.9 us -> 33.2 us  [local(): pl.pallas_call(forecast_kernel, out_shape=(vmem((F, R, M, C), f32), vmem(...]
    pallas_call x1, Pallas kernels: 2.7 us -> 2.14 us  [local(): pl.pallas_call(analysis_kernel, out_shape=jax.ShapeDtypeStruct((F, M, R,...]
where the time goes in v5:
time: 35.5 us; the launch traced here: 35.4 us
  Pallas kernels  35.4 us (100%)
    pallas_call x1, Pallas kernels, local(): pl.pallas_call(forecast_kernel, out_shape=(vmem((F, R, M, C), f32), vmem(...  33.2 us
    pallas_call x1, Pallas kernels, local(): pl.pallas_call(analysis_kernel, out_shape=jax.ShapeDtypeStruct((F, M, R,...  2.14 us

profile of v5, /device:TPU:1, one launch (start us, length us, event | category | flops | bytes accessed | tf_op | source)
XLA Modules:
  0.0 35.4 jit_solution(10891734329088833376)
XLA Ops:
  0.0 33.2 %forecast_and_transform.1 = (f32[2,32,32,256]{3,2,1,0:T(8,128)S(1)}, f32[32,128]{1,0:T(8,128)S(1)}) custom-call(f32[2,1024,256]{2,1,0:T(8,128)} %bitcast.2, f32[32,256]{1,0:T(8,128)} %cx_in.1, f32[32,256]{1,0:T(8,128)} %cy_in.1, f32[2]{0:T(128)} %diff_in.1, s32[2,1024]{1,0:T(2,128)} %cell_in.1, f32[2,1024]{1,0:T(2,128)} %value_in.1, f32[2,32,1024]{2,1,0:T(8,128)} %bitcast.3, ...), custom_call_target="tpu_custom_call" | custom-call | tf_op jit(solution)/shard_map/forecast_and_transform/pallas_call | solution.py:471
  33.3 2.1 %analysis.1 = f32[2,32,32,256]{3,2,1,0:T(8,128)} custom-call(f32[32,128]{1,0:T(8,128)S(1)} %get-tuple-element.7.e_ref, f32[2,32,32,256]{3,2,1,0:T(8,128)S(1)} %get-tuple-element.8.x), custom_call_target="tpu_custom_call" | custom-call | tf_op jit(solution)/shard_map/analysis/pallas_call | solution.py:516

commit v6 on v5

--- a/solution.py
+++ b/solution.py
@@ -14,8 +14,8 @@
 GROUP = 16
 REACH = tuple(sorted(((di, dj) for di in (-1, 0, 1) for dj in range(-2, 3) if (di, dj) != (0, 0)), key=lambda d: -abs(d[0]) * 3 - abs(d[1])))
 ADJACENT = tuple(d for d in REACH if abs(d[1]) < 2)
-ROWS, COLS, CORNER, CROWS, CCOLS = 0, 2, 4, 5, 6
-CHANNELS = 7
+ROWS, COLS, CORNER, CROWS, CCOLS, NEAR = 0, 2, 4, 5, 6, 7
+CHANNELS = 8
 
 
 def iota(shape, axis):
@@ -24,6 +24,10 @@
 
 def dot(a, b):
     return lax.dot_general(a, b, (((1,), (0,)), ((), ())), precision=HI, preferred_element_type=jnp.float32)
+
+
+def dot_t(a, b):
+    return lax.dot_general(a, b, (((1,), (1,)), ((), ())), precision=HI, preferred_element_type=jnp.float32)
 
 
 def eliminate(system):
@@ -60,7 +64,7 @@
 def forecast_kernel(
     ens, cx_in, cy_in, diff_in, cell_in, value_in, noise_in, var_in,
     x2, e_out,
-    halves, q, x1, own_w, own_e, far, next_w, next_e, corner_s, corner_r, crow_s, crow_r, ccol_s, ccol_r,
+    halves, q, x1, own_w, own_e, far, next_w, next_e, corner_s, corner_r, corner_t, near_s, near_r, crow_s, crow_r, ccol_s, ccol_r,
     fix_w, fix_e, coef, courant, diff, cell, cell16, value, noise, picks, id_v, id_s, msg, got,
     in_sem, p1_send, p1_recv, p2_send, p2_recv,
 ):
@@ -82,13 +86,13 @@
     def loaded(dst, sem):
         pltpu.make_async_copy(dst, dst, in_sem.at[sem]).wait()
 
+    cell_copy = load(cell_in, cell, 3)
+    load(cx_in, courant.at[0], 1)
+    load(cy_in, courant.at[1], 1)
     for f in range(F):
         for h in range(2):
             load(ens.at[f, :, pl.ds(h * H, H)], halves.at[h, f], 0)
-    load(cx_in, courant.at[0], 1)
-    load(cy_in, courant.at[1], 1)
     diff_copy = load(diff_in, diff, 2)
-    cell_copy = load(cell_in, cell, 3)
     load(value_in, value.at[0], 4)
     load(var_in, value.at[1], 4)
     noise_copy = load(noise_in, noise, 5)
@@ -107,6 +111,52 @@
 
     def came(dst, channel):
         pltpu.make_async_copy(dst, dst, p1_recv.at[channel]).wait()
+
+    count = cell.shape[1]
+    chunks = count // H
+    wide = lo * C
+    shift = wide.bit_length() - 1
+    n_rows = BATCHES * chunks
+    cell_copy.wait()
+    for ch in range(chunks):
+        cell16[BATCHES * ch : BATCHES * (ch + 1), :] = cell[:, ch * H : (ch + 1) * H]
+    cells = cell16[...]
+    l_col = (cells & (wide - 1)) - me_j * C
+    tiles = (0, 1, -1)
+    masks, codes = [], []
+    for di in tiles:
+        l_row = lax.shift_right_logical(cells, shift) - lax.rem(me_i + (di + la), la) * R
+        mine = (l_row >= 0) & (l_row < R) & (l_col >= 0) & (l_col < C)
+        masks.append(jnp.where(mine, 1.0, 0.0))
+        codes.append(jnp.where(mine, l_row * C + l_col, 0).astype(jnp.float32))
+    mask = jnp.concatenate(masks, axis=0)
+    all_rows = len(tiles) * n_rows
+    before = jnp.where(iota((H, H), 0) < iota((H, H), 1), 1.0, 0.0)
+    ii, jj = iota((all_rows, all_rows), 0), iota((all_rows, all_rows), 1)
+    related = (lax.rem(ii, BATCHES) == lax.rem(jj, BATCHES)) & (lax.div(ii, n_rows) == lax.div(jj, n_rows))
+    rows_before = jnp.where(related & (jj < ii), 1.0, 0.0)
+    totals = jnp.broadcast_to(jnp.sum(mask, axis=1, keepdims=True), (all_rows, H))
+    rank = dot(mask, before) + dot(rows_before, totals)
+    rank = jnp.where(mask > 0.5, rank, -1.0).astype(jnp.int32)
+    slot = iota((SLOTS, H), 0)
+    slot_lane = iota((SLOTS, H), 1)
+    slot_wide = iota((SLOTS, C), 1)
+    chosen, own_code, columns = [], [], []
+    for n, di in enumerate(tiles):
+        for b in range(BATCHES):
+            rows_b = [BATCHES * ch + b for ch in range(chunks)]
+            picked = [jnp.broadcast_to(rank[n * n_rows + k : n * n_rows + k + 1, :], (SLOTS, H)) == slot for k in rows_b]
+            total = jnp.zeros((SLOTS, H), jnp.float32)
+            for here, k in zip(picked, rows_b):
+                total = jnp.where(here, jnp.broadcast_to(codes[n][k : k + 1, :], (SLOTS, H)), total)
+            code_b = jnp.sum(total, axis=1, keepdims=True).astype(jnp.int32)
+            columns.append(jnp.broadcast_to(code_b & (C - 1), (SLOTS, C)))
+            if di == 0:
+                chosen.append(jnp.concatenate([jnp.where(here, 1.0, 0.0) for here in picked], axis=1))
+                own_code.append(jnp.concatenate([codes[n][k : k + 1, :] for k in rows_b], axis=1))
+
+    def hot(n, b, by=0):
+        return jnp.where(slot_wide == columns[BATCHES * n + b] + by, 1.0, 0.0)
 
     loaded(courant, 1)
     diff_copy.wait()
@@ -159,56 +209,43 @@
     def send_field(f):
         send(COLS + f, own_e.at[f], far.at[f, 0], at(0, 1))
         send(COLS + f, own_w.at[f], far.at[f, 1], at(0, -1))
+
+    def send_rows(f):
         send(ROWS + f, q.at[f, pl.ds(R, 2)], q.at[f, pl.ds(0, 2)], at(1, 0))
         send(ROWS + f, q.at[f, pl.ds(2, 2)], q.at[f, pl.ds(R + 2, 2)], at(-1, 0))
 
     pack(0)
     pack(1)
+    none = jnp.zeros((2 * M, C), jnp.float32)
+    for side, (outer, inner_row) in enumerate(((R + 1, R), (2, 3))):
+        out = jnp.zeros((M, H), jnp.float32)
+        for b in range(BATCHES):
+            spots = jnp.concatenate([hot(side + 1, b, by) for by in (-1, 0, 1, 0)], axis=0)
+            spots = jnp.concatenate([spots, none] if b == 0 else [none, spots], axis=0)
+            both = dot_t(jnp.concatenate([q[b % F, outer], q[b % F, inner_row]], axis=0), spots)
+            out = out + jnp.where((lane & 63) < 48, both[0:M], both[M : 2 * M])
+        near_s[side] = out
     pl.semaphore_wait(barrier, len(ADJACENT))
     for n, target in enumerate(((1, 1), (1, -1), (-1, 1), (-1, -1))):
         send(CORNER, corner_s, corner_r.at[n], at(*target))
+    send(NEAR, near_s.at[0], near_r.at[0], at(1, 0))
+    send(NEAR, near_s.at[1], near_r.at[1], at(-1, 0))
     send(CROWS, crow_s.at[0], crow_r.at[0], at(1, 0))
     send(CROWS, crow_s.at[1], crow_r.at[1], at(-1, 0))
     send(CCOLS, ccol_s.at[0], ccol_r.at[0], at(0, 1))
     send(CCOLS, ccol_s.at[1], ccol_r.at[1], at(0, -1))
     send_field(0)
-
-    cell_copy.wait()
+    send_field(1)
+
     loaded(value, 4)
-    count = cell.shape[1]
-    chunks = count // H
-    wide = lo * C
-    shift = wide.bit_length() - 1
-    n_rows = BATCHES * chunks
-    for ch in range(chunks):
-        cell16[BATCHES * ch : BATCHES * (ch + 1), :] = cell[:, ch * H : (ch + 1) * H]
-    cells = cell16[...]
-    l_row = lax.shift_right_logical(cells, shift) - me_i * R
-    l_col = (cells & (wide - 1)) - me_j * C
-    mine = (l_row >= 0) & (l_row < R) & (l_col >= 0) & (l_col < C)
-    mask = jnp.where(mine, 1.0, 0.0)
-    before = jnp.where(iota((H, H), 0) < iota((H, H), 1), 1.0, 0.0)
-    ii, jj = iota((n_rows, n_rows), 0), iota((n_rows, n_rows), 1)
-    rows_before = jnp.where((lax.rem(ii, BATCHES) == lax.rem(jj, BATCHES)) & (jj < ii), 1.0, 0.0)
-    totals = jnp.broadcast_to(jnp.sum(mask, axis=1, keepdims=True), (n_rows, H))
-    rank = dot(mask, before) + dot(rows_before, totals)
-    rank = jnp.where(mine, rank, -1.0).astype(jnp.int32)
-    code = jnp.where(mine, l_row * C + l_col, 0).astype(jnp.float32)
-    slot = iota((SLOTS, H), 0)
     noise_copy.wait()
     picks[...] = jnp.zeros((BATCHES, M + 8, H), jnp.float32)
     sub_wide = iota((8, count), 0)
     for b in range(BATCHES):
-        rows_b = [BATCHES * ch + b for ch in range(chunks)]
-        chosen = [jnp.where(jnp.broadcast_to(rank[n : n + 1, :], (SLOTS, H)) == slot, 1.0, 0.0) for n in rows_b]
-        code_b = jnp.concatenate([code[n : n + 1, :] for n in rows_b], axis=1)
         more = jnp.where(sub_wide == 0, jnp.broadcast_to(value[0, b : b + 1, :], (8, count)), 0.0)
         more = jnp.where(sub_wide == 1, jnp.broadcast_to(value[1, b : b + 1, :], (8, count)), more)
-        more = jnp.where(sub_wide == 2, jnp.broadcast_to(code_b, (8, count)), more)
-        picks[b, :, 0:SLOTS] = lax.dot_general(
-            jnp.concatenate([noise[b], more], axis=0), jnp.concatenate(chosen, axis=1),
-            (((1,), (1,)), ((), ())), precision=HI, preferred_element_type=jnp.float32,
-        )
+        more = jnp.where(sub_wide == 2, jnp.broadcast_to(own_code[b], (8, count)), more)
+        picks[b, :, 0:SLOTS] = dot_t(jnp.concatenate([noise[b], more], axis=0), chosen[b])
         id_v[b] = (picks[b, M : M + 8, :] + 0.5).astype(jnp.int32)
     id_copy = load(id_v, id_s, 6)
 
@@ -273,8 +310,9 @@
         row_step(src, dst, f, R - 1, src_at, dst_at, None, north=False)
 
     inner(0, q, x1, 2, 1)
-    send_field(1)
+    send_rows(0)
     inner(0, x1, x2, 1, 0)
+    send_rows(1)
     id_copy.wait()
     ids = [[id_s[b, 2, s] for s in range(SLOTS)] for b in range(BATCHES)]
 
@@ -285,8 +323,44 @@
         for side, first in ((0, 0), (1, 8 + R)):
             p = halo_rows[side]
             set_coef(f, first, [centre_of(p, rates[f])] + [part + rates[f] for part in p])
-    came(corner_r, CORNER)
-    corners = jnp.concatenate([corner_r[n] for n in range(4)] + [jnp.zeros((H - 32, H), jnp.float32)], axis=0).T
+
+    def near_weights(b):
+        f = b % F
+
+        def row_of(n, r):
+            return jnp.concatenate([coef[f, n, h, r + 8 : r + 9, :] for h in range(2)], axis=1)
+
+        at_first, at_last = iota((1, C), 1) == 0, iota((1, C), 1) == C - 1
+        rows = []
+        for n, back, row, halo, inner_row in ((3, 4, 0, -1, 1), (4, 3, R - 1, R, R - 2)):
+            edge = row_of(n, row)
+            from_w = jnp.where(at_first, 0.0, pltpu.roll(edge, 1, 1))
+            from_e = jnp.where(at_last, 0.0, pltpu.roll(edge, C - 1, 1))
+            rows += [
+                edge * row_of(1, halo) + row_of(1, row) * from_w,
+                edge * row_of(0, halo) + row_of(0, row) * edge,
+                edge * row_of(2, halo) + row_of(2, row) * from_e,
+                edge * row_of(n, halo),
+                edge * row_of(back, halo),
+                row_of(n, inner_row) * edge,
+            ]
+        pad = jnp.zeros((H - SLOTS, C), jnp.float32)
+        spots = jnp.concatenate([hot(0, b), pad], axis=0)
+        sub = iota((16, C), 0)
+        stacked = jnp.zeros((16, C), jnp.float32)
+        for k, row in enumerate(rows):
+            stacked = jnp.where(sub == k, jnp.broadcast_to(row, (16, C)), stacked)
+        weights = dot_t(stacked, spots)
+        own = dot_t(jnp.concatenate([q[f, 2], q[f, R + 1]], axis=0), spots)
+        code_row = id_v[b, 2:3, :]
+        at_row = lax.shift_right_logical(code_row, 8) & (R - 1)
+        out = []
+        for side, (row, inner_row) in enumerate(((0, 1), (R - 1, R - 2))):
+            w = [weights[6 * side + k : 6 * side + k + 1, :] for k in range(6)]
+            w = [jnp.where(at_row == row, v, 0.0) for v in w[:5]] + [jnp.where(at_row == inner_row, w[5], 0.0)]
+            out.append((w[0], w[1] + w[5], w[2], w[3], w[4] * own[side * M : (side + 1) * M]))
+        return out
+
     lane_row = iota((1, H), 1)
 
     def packed_rates(f, ref, side):
@@ -297,13 +371,7 @@
 
     def halo_columns(f):
         came(far.at[f], COLS + f)
-        corner = [jnp.broadcast_to(corners[f * M : (f + 1) * M, n : n + 1], (M, H)) for n in (3, 10, 17, 24)]
-        west = far[f, 0]
-        west = jnp.where(lane == H - 1, corner[0], jnp.where(lane == 2 * R + 1, corner[2], west))
-        east = far[f, 1]
-        east = jnp.where(lane == H - 2, corner[1], jnp.where(lane == 2 * R, corner[3], east))
-        far[f, 0] = west
-        far[f, 1] = east
+        west, east = far[f, 0], far[f, 1]
         sides = (
             (next_w, west, pltpu.roll(west, 1, 1), pltpu.roll(own_w[f], 1, 1)),
             (next_e, east, pltpu.roll(own_e[f], H - 1, 1), pltpu.roll(east, H - 1, 1)),
@@ -313,6 +381,44 @@
             out = rate[0] * c + rate[1] * w + rate[2] * e
             out = out + rate[3] * pltpu.roll(c, 2, 1) + rate[4] * pltpu.roll(c, H - 2, 1)
             to[f] = jnp.where(lane < 2 * R, out, 0.0)
+
+    def corner_rates(f):
+        halo_w, halo_e = packed_rates(f, ccol_r, 0), packed_rates(f, ccol_r, 1)
+        west, east = packed_rates(f, ccol_s, 1)[1], packed_rates(f, ccol_s, 0)[2]
+        w = west * pltpu.roll(jnp.where(lane_row < R, halo_w[3], halo_w[4]), H - 1, 1)
+        e = east * pltpu.roll(jnp.where(lane_row < R, halo_e[3], halo_e[4]), 1, 1)
+        w = jnp.where((lane_row == 0) | (lane_row == 2 * R - 2), w, 0.0)
+        e = jnp.where((lane_row == 1) | (lane_row == 2 * R - 1), e, 0.0)
+        return w, e
+
+    near = [near_weights(b) for b in range(BATCHES)]
+    beyond = [corner_rates(f) for f in range(F)]
+
+    def corner_weights(b):
+        code_row = id_v[b, 2:3, :]
+        at_row, at_col = lax.shift_right_logical(code_row, 8) & (R - 1), code_row & (C - 1)
+        west, east = beyond[b % F]
+        out = []
+        for side, (row, at) in enumerate(((0, 0), (R - 1, 2 * R - 2))):
+            w = near[b][side]
+            through_w, through_e = west[:, at : at + 1], east[:, at + 1 : at + 2]
+            out.append(jnp.where(at_col == 0, w[0] + jnp.where(at_row == row, through_w, 0.0), 0.0))
+            out.append(jnp.where(at_col == C - 1, w[2] + jnp.where(at_row == row, through_e, 0.0), 0.0))
+        return out
+
+    corner_part = [corner_weights(b) for b in range(BATCHES)]
+
+    def corner_columns(f):
+        turned = corner_t[...]
+        return [jnp.broadcast_to(turned[f * M : (f + 1) * M, n : n + 1], (M, H)) for n in (3, 10, 17, 24)]
+
+    def late_corners(f):
+        south_w, south_e, north_w, north_e = corner_columns(f)
+        far[f, 0] = jnp.where(lane == H - 1, south_w, jnp.where(lane == 2 * R + 1, north_w, far[f, 0]))
+        far[f, 1] = jnp.where(lane == H - 2, south_e, jnp.where(lane == 2 * R, north_e, far[f, 1]))
+        west, east = beyond[f]
+        fix_w[f] = fix_w[f] + west * jnp.where(lane < R, south_w, north_w)
+        fix_e[f] = fix_e[f] + east * jnp.where(lane < R, south_e, north_e)
 
     def fix_columns(f):
         inside = lane < 2 * R
@@ -346,6 +452,15 @@
                     x2[f, inner_row, :, cut] + coef[f, n, h, inner_row + 8 : inner_row + 9, :] * t[h]
                 )
 
+    def near_rows(b):
+        total = jnp.zeros((M, H), jnp.float32)
+        for side in range(2):
+            got_rows = near_r[side]
+            g = [pltpu.roll(got_rows, (2 * H - 64 * b - SLOTS * k) % H, 1) for k in range(4)]
+            w = near[b][side]
+            total = total + w[0] * g[0] + w[1] * g[1] + w[2] * g[2] + w[3] * g[3] + w[4]
+        return total
+
     def unpack_columns(f):
         def body(r):
             west = pltpu.roll(fix_w[f], (H - 2 * r) & (H - 1), 1)
@@ -355,7 +470,7 @@
 
         rows_of(body, 0, R)
 
-    def observe(b):
+    def see(b):
         f = b % F
         seen = jnp.zeros((M, H), jnp.float32)
         for s in range(SLOTS):
@@ -368,6 +483,11 @@
             spot_e = jnp.where(col >= C - 2, 2 * at_row + col - (C - 2), -1)
             picked = picked + jnp.where(lane == spot_w, fix_w[f], 0.0) + jnp.where(lane == spot_e, fix_e[f], 0.0)
             seen = jnp.where(lane == s, jnp.broadcast_to(jnp.sum(picked, axis=1, keepdims=True), (M, H)), seen)
+        return seen
+
+    def observe(b, seen):
+        for weight, column in zip(corner_part[b], corner_columns(b % F)):
+            seen = seen + weight * column
         mean = jnp.sum(seen, axis=0, keepdims=True) * (1.0 / M)
         var_b = picks[b, M + 1 : M + 2, :]
         there = var_b > 0.0
@@ -409,22 +529,30 @@
 
     halo_columns(0)
     fix_columns(0)
-    fix_rows(0)
-    tell(0, observe(0))
+    seen0 = see(0)
+    came(near_r, NEAR)
+    seen0 = seen0 + near_rows(0)
+    came(corner_r, CORNER)
+    corner_t[...] = jnp.concatenate([corner_r[n] for n in range(4)] + [jnp.zeros((H - 32, H), jnp.float32)], axis=0).T
+    tell(0, observe(0, seen0))
     inner(1, q, x1, 2, 1)
     inner(1, x1, x2, 1, 0)
     halo_columns(1)
     fix_columns(1)
-    fix_rows(1)
-    r1 = observe(1)
+    r1 = observe(1, see(1) + near_rows(1))
     solved0 = transform(0)
     w0 = jnp.where(lane < M, pltpu.roll(solved0, H - M, 1), 0.0)
     w0_mean = jnp.sum(w0, axis=1, keepdims=True) * (1.0 / M)
     both0 = jnp.where(lane < M, w0 - w0_mean, jnp.where(lane < 2 * M, -solved0, 0.0))
     tell(1, r1 + dot(r1[:, 0:M], both0))
     c0 = centered_rows(solved0)
+    late_corners(0)
+    late_corners(1)
     unpack_columns(0)
     unpack_columns(1)
+    fix_rows(0)
+    fix_rows(1)
+    sent(near_s, NEAR)
     for f in range(F):
         sent(q.at[f, pl.ds(2, 4)], ROWS + f)
         sent(far.at[f], COLS + f)
@@ -484,6 +612,9 @@
             vmem((F, M, H), f32),
             vmem((8, H), f32),
             vmem((4, 8, H), f32),
+            vmem((H, H), f32),
+            vmem((2, M, H), f32),
+            vmem((2, M, H), f32),
             vmem((2, 8, C), f32),
             vmem((2, 8, C), f32),
             vmem((2, 8, H), f32),

time: 35.5 us -> 35.2 us (level)
  no operation moved by 1% of the time
where the time goes in v6:
time: 35.2 us; the launch traced here: 35.1 us
  Pallas kernels  35.1 us (100%)
    pallas_call x1, Pallas kernels, local(): pl.pallas_call(forecast_kernel, out_shape=(vmem((F, R, M, C), f32), vmem(...  32.9 us
    pallas_call x1, Pallas kernels, local(): pl.pallas_call(analysis_kernel, out_shape=jax.ShapeDtypeStruct((F, M, R,...  2.14 us

profile of v6, /device:TPU:1, one launch (start us, length us, event | category | flops | bytes accessed | tf_op | source)
XLA Modules:
  0.0 35.1 jit_solution(4899360658762637950)
XLA Ops:
  0.0 32.9 %forecast_and_transform.1 = (f32[2,32,32,256]{3,2,1,0:T(8,128)S(1)}, f32[32,128]{1,0:T(8,128)S(1)}) custom-call(f32[2,1024,256]{2,1,0:T(8,128)} %bitcast.2, f32[32,256]{1,0:T(8,128)} %cx_in.1, f32[32,256]{1,0:T(8,128)} %cy_in.1, f32[2]{0:T(128)} %diff_in.1, s32[2,1024]{1,0:T(2,128)} %cell_in.1, f32[2,1024]{1,0:T(2,128)} %value_in.1, f32[2,32,1024]{2,1,0:T(8,128)} %bitcast.3, ...), custom_call_target="tpu_custom_call" | custom-call | tf_op jit(solution)/shard_map/forecast_and_transform/pallas_call | solution.py:599
  32.9 2.1 %analysis.1 = f32[2,32,32,256]{3,2,1,0:T(8,128)} custom-call(f32[32,128]{1,0:T(8,128)S(1)} %get-tuple-element.7.e_ref, f32[2,32,32,256]{3,2,1,0:T(8,128)S(1)} %get-tuple-element.8.x), custom_call_target="tpu_custom_call" | custom-call | tf_op jit(solution)/shard_map/analysis/pallas_call | solution.py:647

commit v7 on v6

--- a/solution.py
+++ b/solution.py
@@ -11,7 +11,7 @@
 H = 128
 SLOTS = 16
 BATCHES = 2
-GROUP = 16
+GROUP = 32
 REACH = tuple(sorted(((di, dj) for di in (-1, 0, 1) for dj in range(-2, 3) if (di, dj) != (0, 0)), key=lambda d: -abs(d[0]) * 3 - abs(d[1])))
 ADJACENT = tuple(d for d in REACH if abs(d[1]) < 2)
 ROWS, COLS, CORNER, CROWS, CCOLS, NEAR = 0, 2, 4, 5, 6, 7
@@ -202,7 +202,7 @@
             return west, east
 
         zero = jnp.zeros((M, H), jnp.float32)
-        west, east = lax.fori_loop(0, R, body, (zero, zero), unroll=8)
+        west, east = lax.fori_loop(0, R, body, (zero, zero), unroll=R)
         own_w[f] = west
         own_e[f] = east
 
@@ -215,14 +215,17 @@
         send(ROWS + f, q.at[f, pl.ds(2, 2)], q.at[f, pl.ds(R + 2, 2)], at(-1, 0))
 
     pack(0)
-    pack(1)
+
+    def edge_row(f, r):
+        return jnp.concatenate([halves[h, f, pl.ds(r, M, stride=R), :] for h in range(2)], axis=1)
+
     none = jnp.zeros((2 * M, C), jnp.float32)
-    for side, (outer, inner_row) in enumerate(((R + 1, R), (2, 3))):
+    for side, (outer, inner_row) in enumerate(((R - 1, R - 2), (0, 1))):
         out = jnp.zeros((M, H), jnp.float32)
         for b in range(BATCHES):
             spots = jnp.concatenate([hot(side + 1, b, by) for by in (-1, 0, 1, 0)], axis=0)
             spots = jnp.concatenate([spots, none] if b == 0 else [none, spots], axis=0)
-            both = dot_t(jnp.concatenate([q[b % F, outer], q[b % F, inner_row]], axis=0), spots)
+            both = dot_t(jnp.concatenate([edge_row(b % F, outer), edge_row(b % F, inner_row)], axis=0), spots)
             out = out + jnp.where((lane & 63) < 48, both[0:M], both[M : 2 * M])
         near_s[side] = out
     pl.semaphore_wait(barrier, len(ADJACENT))
@@ -235,6 +238,7 @@
     send(CCOLS, ccol_s.at[0], ccol_r.at[0], at(0, 1))
     send(CCOLS, ccol_s.at[1], ccol_r.at[1], at(0, -1))
     send_field(0)
+    pack(1)
     send_field(1)
 
     loaded(value, 4)
@@ -298,11 +302,8 @@
         row_step(q, x1, f, r, 2, 1, (far[f, 0], far[f, 1]))
 
     def rows_of(step, begin, end):
-        def body(r, carry):
+        for r in range(begin, end):
             step(r)
-            return carry
-
-        lax.fori_loop(begin, end, body, 0, unroll=2)
 
     def inner(f, src, dst, src_at, dst_at):
         row_step(src, dst, f, 0, src_at, dst_at, None, south=False)
@@ -317,7 +318,6 @@
     ids = [[id_s[b, 2, s] for s in range(SLOTS)] for b in range(BATCHES)]
 
     came(crow_r, CROWS)
-    came(ccol_r, CCOLS)
     halo_rows = [parts_of(crow_r[side, 0:1, :], crow_r[side, 1:2, :]) for side in range(2)]
     for f in range(F):
         for side, first in ((0, 0), (1, 8 + R)):
@@ -382,6 +382,15 @@
             out = out + rate[3] * pltpu.roll(c, 2, 1) + rate[4] * pltpu.roll(c, H - 2, 1)
             to[f] = jnp.where(lane < 2 * R, out, 0.0)
 
+    def near_rows(b):
+        total = jnp.zeros((M, H), jnp.float32)
+        for side in range(2):
+            got_rows = near_r[side]
+            g = [pltpu.roll(got_rows, (2 * H - 64 * b - SLOTS * k) % H, 1) for k in range(4)]
+            w = near[b][side]
+            total = total + w[0] * g[0] + w[1] * g[1] + w[2] * g[2] + w[3] * g[3] + w[4]
+        return total
+
     def corner_rates(f):
         halo_w, halo_e = packed_rates(f, ccol_r, 0), packed_rates(f, ccol_r, 1)
         west, east = packed_rates(f, ccol_s, 1)[1], packed_rates(f, ccol_s, 0)[2]
@@ -392,6 +401,9 @@
         return w, e
 
     near = [near_weights(b) for b in range(BATCHES)]
+    came(near_r, NEAR)
+    rows0 = near_rows(0)
+    came(ccol_r, CCOLS)
     beyond = [corner_rates(f) for f in range(F)]
 
     def corner_weights(b):
@@ -452,15 +464,6 @@
                     x2[f, inner_row, :, cut] + coef[f, n, h, inner_row + 8 : inner_row + 9, :] * t[h]
                 )
 
-    def near_rows(b):
-        total = jnp.zeros((M, H), jnp.float32)
-        for side in range(2):
-            got_rows = near_r[side]
-            g = [pltpu.roll(got_rows, (2 * H - 64 * b - SLOTS * k) % H, 1) for k in range(4)]
-            w = near[b][side]
-            total = total + w[0] * g[0] + w[1] * g[1] + w[2] * g[2] + w[3] * g[3] + w[4]
-        return total
-
     def unpack_columns(f):
         def body(r):
             west = pltpu.roll(fix_w[f], (H - 2 * r) & (H - 1), 1)
@@ -530,8 +533,7 @@
     halo_columns(0)
     fix_columns(0)
     seen0 = see(0)
-    came(near_r, NEAR)
-    seen0 = seen0 + near_rows(0)
+    seen0 = seen0 + rows0
     came(corner_r, CORNER)
     corner_t[...] = jnp.concatenate([corner_r[n] for n in range(4)] + [jnp.zeros((H - 32, H), jnp.float32)], axis=0).T
     tell(0, observe(0, seen0))

time: 35.2 us -> 34.3 us (0.974)
  Pallas kernels: 35.1 us -> 34.2 us
    pallas_call x1, Pallas kernels: 32.9 us -> 32.2 us  [local(): pl.pallas_call(forecast_kernel, out_shape=(vmem((F, R, M, C), f32), vmem(...]
where the time goes in v7:
time: 34.3 us; the launch traced here: 34.2 us
  Pallas kernels  34.2 us (100%)
    pallas_call x1, Pallas kernels, local(): pl.pallas_call(forecast_kernel, out_shape=(vmem((F, R, M, C), f32), vmem(...  32.2 us
    pallas_call x1, Pallas kernels, local(): pl.pallas_call(analysis_kernel, out_shape=jax.ShapeDtypeStruct((F, M, R,...  1.95 us

profile of v7, /device:TPU:1, one launch (start us, length us, event | category | flops | bytes accessed | tf_op | source)
XLA Modules:
  0.0 34.2 jit_solution(16066172513858283174)
XLA Ops:
  0.0 32.2 %forecast_and_transform.1 = (f32[2,32,32,256]{3,2,1,0:T(8,128)S(1)}, f32[32,128]{1,0:T(8,128)S(1)}) custom-call(f32[2,1024,256]{2,1,0:T(8,128)} %bitcast.2, f32[32,256]{1,0:T(8,128)} %cx_in.1, f32[32,256]{1,0:T(8,128)} %cy_in.1, f32[2]{0:T(128)} %diff_in.1, s32[2,1024]{1,0:T(2,128)} %cell_in.1, f32[2,1024]{1,0:T(2,128)} %value_in.1, f32[2,32,1024]{2,1,0:T(8,128)} %bitcast.3, ...), custom_call_target="tpu_custom_call" | custom-call | tf_op jit(solution)/shard_map/forecast_and_transform/pallas_call | solution.py:601
  32.2 2.0 %analysis.1 = f32[2,32,32,256]{3,2,1,0:T(8,128)} custom-call(f32[32,128]{1,0:T(8,128)S(1)} %get-tuple-element.7.e_ref, f32[2,32,32,256]{3,2,1,0:T(8,128)S(1)} %get-tuple-element.8.x), custom_call_target="tpu_custom_call" | custom-call | tf_op jit(solution)/shard_map/analysis/pallas_call | solution.py:649

commit v8 on v7

--- a/solution.py
+++ b/solution.py
@@ -317,12 +317,6 @@
     id_copy.wait()
     ids = [[id_s[b, 2, s] for s in range(SLOTS)] for b in range(BATCHES)]
 
-    came(crow_r, CROWS)
-    halo_rows = [parts_of(crow_r[side, 0:1, :], crow_r[side, 1:2, :]) for side in range(2)]
-    for f in range(F):
-        for side, first in ((0, 0), (1, 8 + R)):
-            p = halo_rows[side]
-            set_coef(f, first, [centre_of(p, rates[f])] + [part + rates[f] for part in p])
 
     def near_weights(b):
         f = b % F
@@ -344,14 +338,12 @@
                 edge * row_of(back, halo),
                 row_of(n, inner_row) * edge,
             ]
-        pad = jnp.zeros((H - SLOTS, C), jnp.float32)
-        spots = jnp.concatenate([hot(0, b), pad], axis=0)
         sub = iota((16, C), 0)
         stacked = jnp.zeros((16, C), jnp.float32)
         for k, row in enumerate(rows):
             stacked = jnp.where(sub == k, jnp.broadcast_to(row, (16, C)), stacked)
-        weights = dot_t(stacked, spots)
-        own = dot_t(jnp.concatenate([q[f, 2], q[f, R + 1]], axis=0), spots)
+        weights = dot_t(stacked, spots[b])
+        own = own_edges[b]
         code_row = id_v[b, 2:3, :]
         at_row = lax.shift_right_logical(code_row, 8) & (R - 1)
         out = []
@@ -400,9 +392,10 @@
         e = jnp.where((lane_row == 1) | (lane_row == 2 * R - 1), e, 0.0)
         return w, e
 
-    near = [near_weights(b) for b in range(BATCHES)]
-    came(near_r, NEAR)
-    rows0 = near_rows(0)
+    near = [None] * BATCHES
+    pad = jnp.zeros((H - SLOTS, C), jnp.float32)
+    spots = [jnp.concatenate([hot(0, b), pad], axis=0) for b in range(BATCHES)]
+    own_edges = [dot_t(jnp.concatenate([q[b % F, 2], q[b % F, R + 1]], axis=0), spots[b]) for b in range(BATCHES)]
     came(ccol_r, CCOLS)
     beyond = [corner_rates(f) for f in range(F)]
 
@@ -418,7 +411,7 @@
             out.append(jnp.where(at_col == C - 1, w[2] + jnp.where(at_row == row, through_e, 0.0), 0.0))
         return out
 
-    corner_part = [corner_weights(b) for b in range(BATCHES)]
+    corner_part = [None] * BATCHES
 
     def corner_columns(f):
         turned = corner_t[...]
@@ -533,10 +526,21 @@
     halo_columns(0)
     fix_columns(0)
     seen0 = see(0)
-    seen0 = seen0 + rows0
+    came(crow_r, CROWS)
+    halo_rows = [parts_of(crow_r[side, 0:1, :], crow_r[side, 1:2, :]) for side in range(2)]
+    for f in range(F):
+        for side, first in ((0, 0), (1, 8 + R)):
+            p = halo_rows[side]
+            set_coef(f, first, [centre_of(p, rates[f])] + [part + rates[f] for part in p])
+    near[0] = near_weights(0)
+    corner_part[0] = corner_weights(0)
+    came(near_r, NEAR)
+    seen0 = seen0 + near_rows(0)
     came(corner_r, CORNER)
     corner_t[...] = jnp.concatenate([corner_r[n] for n in range(4)] + [jnp.zeros((H - 32, H), jnp.float32)], axis=0).T
     tell(0, observe(0, seen0))
+    near[1] = near_weights(1)
+    corner_part[1] = corner_weights(1)
     inner(1, q, x1, 2, 1)
     inner(1, x1, x2, 1, 0)
     halo_columns(1)

time: 34.3 us -> 34.3 us (level)
  no operation moved by 1% of the time
where the time goes in v8:
time: 34.3 us; the launch traced here: 34.2 us
  Pallas kernels  34.2 us (100%)
    pallas_call x1, Pallas kernels, local(): pl.pallas_call(forecast_kernel, out_shape=(vmem((F, R, M, C), f32), vmem(...  32.2 us
    pallas_call x1, Pallas kernels, local(): pl.pallas_call(analysis_kernel, out_shape=jax.ShapeDtypeStruct((F, M, R,...  1.95 us

profile of v8, /device:TPU:1, one launch (start us, length us, event | category | flops | bytes accessed | tf_op | source)
XLA Modules:
  0.0 34.2 jit_solution(5270288254506099747)
XLA Ops:
  0.0 32.2 %forecast_and_transform.1 = (f32[2,32,32,256]{3,2,1,0:T(8,128)S(1)}, f32[32,128]{1,0:T(8,128)S(1)}) custom-call(f32[2,1024,256]{2,1,0:T(8,128)} %bitcast.2, f32[32,256]{1,0:T(8,128)} %cx_in.1, f32[32,256]{1,0:T(8,128)} %cy_in.1, f32[2]{0:T(128)} %diff_in.1, s32[2,1024]{1,0:T(2,128)} %cell_in.1, f32[2,1024]{1,0:T(2,128)} %value_in.1, f32[2,32,1024]{2,1,0:T(8,128)} %bitcast.3, ...), custom_call_target="tpu_custom_call" | custom-call | tf_op jit(solution)/shard_map/forecast_and_transform/pallas_call | solution.py:605
  32.3 2.0 %analysis.1 = f32[2,32,32,256]{3,2,1,0:T(8,128)} custom-call(f32[32,128]{1,0:T(8,128)S(1)} %get-tuple-element.7.e_ref, f32[2,32,32,256]{3,2,1,0:T(8,128)S(1)} %get-tuple-element.8.x), custom_call_target="tpu_custom_call" | custom-call | tf_op jit(solution)/shard_map/analysis/pallas_call | solution.py:653
